TPU v7x, 32 devices: a whole 2x2x4 slice. The times are simulated.
32 devices in a mesh: dp: 8 (over z, x), mp: 4 (over y, core).
Axes of the slice: x: 2, y: 2, z: 4, core: 2. Of those that a mesh axis runs over, the one named last changes fastest.
Arguments:
- char_ids: int32 [1024, 6], P('dp'), may hold values from 0 to 274
- next_chars: int32 [1024, 6], P('dp'), may hold values from 0 to 274
- resets: int32 [1024, 6], P('dp'), may hold values 0 or 1
- embedding: bfloat16 [275, 100], replicated, may hold values from -6 to 6
- input_weight: bfloat16 [100, 4, 2048], P(None, None, 'mp'), may hold values from -0.625 to 0.625
- recurrent_weight: bfloat16 [2048, 4, 2048], P('dp', None, 'mp'), may hold values from -0.125 to 0.125
- gate_bias: float32 [4, 2048], P(None, 'mp'), may hold values from -4 to 4
- decoder_weight: bfloat16 [4, 8, 64, 275], P('mp', 'dp'), may hold values from -1 to 1
- decoder_bias: float32 [275], replicated, may hold values from -4 to 4
Outputs:
- loss: float32 [], replicated
- grad_embedding: float32 [275, 100], replicated
- grad_input_weight: float32 [100, 4, 2048], P(None, None, 'mp')
- grad_recurrent_weight: float32 [2048, 4, 2048], P('dp', None, 'mp')
- grad_gate_bias: float32 [4, 2048], P(None, 'mp')
- grad_decoder_weight: float32 [4, 8, 64, 275], P('mp', 'dp')
- grad_decoder_bias: float32 [275], replicated
Inputs may be any that keep to these rules, and one draw needn't show every extreme that they name: `resets`: 1 marks the first character of a sentence: the state is zeroed before it.
All inputs are finite; a program needn't handle non-finite values. No bound on the sum of `resets` on one device may be relied on, other than what follows from the above.
Results may differ from a plain program's by a relative error of at most 0.0049.
Values may be sent and summed in bfloat16 or wider, within the bound.
A program may use at most 128 MiB of HBM per device.

v0:
```python
import jax
import jax.numpy as jnp
from jax import lax
from jax.sharding import PartitionSpec as P


def on_device(
    char_ids,
    next_chars,
    resets,
    embedding,
    input_weight,
    recurrent_weight,
    gate_bias,
    decoder_weight,
    decoder_bias,
):
    f32 = jnp.float32
    bf16 = jnp.bfloat16
    highest = lax.Precision.HIGHEST
    data_count = lax.axis_size("dp")
    row_count, step_count = char_ids.shape
    vocab_size, width_in = embedding.shape
    local_units = input_weight.shape[2]
    gate_cols = 4 * local_units
    tokens_here = row_count * step_count
    tokens_all = tokens_here * data_count
    gathered_rec, gathered_dec = (
        lax.all_gather(recurrent_weight, "dp", axis=0, tiled=True),
        lax.all_gather(decoder_weight, "dp", axis=1, tiled=True),
    )
    hidden_total = gathered_rec.shape[0]
    rec_matrix = gathered_rec.reshape(hidden_total, gate_cols)
    dec_matrix = gathered_dec.reshape(local_units, vocab_size)
    time_ids = char_ids.T
    keep_mask = (1 - resets.T).astype(f32)
    proj_table = jnp.dot(
        embedding, input_weight.reshape(width_in, gate_cols), preferred_element_type=f32
    )
    projected = jnp.take(proj_table, time_ids, axis=0) + gate_bias.reshape(gate_cols)

    def forward_step(state_pair, inputs):
        hidden_loc, cell_state = state_pair
        proj_now, keep_now = inputs
        hidden_full = lax.all_gather(hidden_loc, "mp", axis=1, tiled=True)
        previous = hidden_full * keep_now[:, None].astype(bf16)
        preact = proj_now + jnp.dot(previous, rec_matrix, preferred_element_type=f32)
        gate_vals = preact.reshape(row_count, 4, local_units)
        in_gate = jax.nn.sigmoid(gate_vals[:, 0])
        forget_gate = jax.nn.sigmoid(gate_vals[:, 1])
        cell_gate = jnp.tanh(gate_vals[:, 2])
        out_gate = jax.nn.sigmoid(gate_vals[:, 3])
        new_cell = forget_gate * cell_state * keep_now[:, None] + in_gate * cell_gate
        new_hidden = (out_gate * jnp.tanh(new_cell)).astype(bf16)
        return ((new_hidden, new_cell), (previous, preact, new_cell, new_hidden))

    first_state = (
        jnp.zeros((row_count, local_units), bf16),
        jnp.zeros((row_count, local_units), f32),
    )
    _, (prevs, preacts, cells, hiddens) = lax.scan(
        forward_step, first_state, (projected, keep_mask)
    )
    flat_hidden = hiddens.reshape(tokens_here, local_units)
    partial_value = jnp.dot(flat_hidden, dec_matrix, preferred_element_type=f32)
    flat_targets = next_chars.T.reshape(tokens_here)
    logit_rows = lax.psum(partial_value, "mp")
    shifted_in = logit_rows + decoder_bias
    row_max = jnp.max(shifted_in, axis=1)
    exp_total = jnp.sum(jnp.exp(shifted_in - row_max[:, None]), axis=1)
    log_total = row_max + jnp.log(exp_total)
    softmax_out = jnp.exp(shifted_in - log_total[:, None])
    onehot = (flat_targets[:, None] == jnp.arange(vocab_size, dtype=jnp.int32)[None, :]).astype(f32)
    picked = jnp.sum(shifted_in * onehot, axis=1)
    grad_rows = ((softmax_out - onehot) / tokens_all).astype(bf16)
    local_loss = jnp.sum(log_total - picked) / tokens_all
    loss_part = jnp.where(lax.axis_index("mp") == 0, local_loss, jnp.zeros((), f32))
    out_grads = jnp.dot(grad_rows, dec_matrix.T, preferred_element_type=f32).reshape(
        step_count, row_count, local_units
    )
    dec_bias_part = jnp.sum(grad_rows.astype(f32), axis=0)
    columns = flat_hidden
    dec_grad = lax.psum_scatter(
        lax.dot_general(columns, grad_rows, (((0,), (0,)), ((), ())), preferred_element_type=f32),
        "dp",
        scatter_dimension=0,
        tiled=True,
    ).reshape(decoder_weight.shape)
    back_matrix = lax.all_gather(recurrent_weight, "dp", axis=0, tiled=True).reshape(
        hidden_total, gate_cols
    )
    prev_cells = (
        jnp.concatenate([jnp.zeros((1, row_count, local_units), f32), cells[:-1]], axis=0)
        * keep_mask[:, :, None]
    )

    def backward_step(state_pair, inputs):
        carry_hidden, carry_cell = state_pair
        preact, cell_state, prev_cell, hidden_out, keep_now = inputs
        gate_vals = preact.reshape(row_count, 4, local_units)
        in_gate = jax.nn.sigmoid(gate_vals[:, 0])
        forget_gate = jax.nn.sigmoid(gate_vals[:, 1])
        cell_gate = jnp.tanh(gate_vals[:, 2])
        out_gate = jax.nn.sigmoid(gate_vals[:, 3])
        hidden_grad = hidden_out + carry_hidden
        squash = jnp.tanh(cell_state)
        cell_grad = hidden_grad * out_gate * (1.0 - squash * squash) + carry_cell
        grad_in = cell_grad * cell_gate * in_gate * (1.0 - in_gate)
        grad_forget = cell_grad * prev_cell * forget_gate * (1.0 - forget_gate)
        grad_cand = cell_grad * in_gate * (1.0 - cell_gate * cell_gate)
        grad_out = hidden_grad * squash * out_gate * (1.0 - out_gate)
        preact_grad = (
            jnp.stack([grad_in, grad_forget, grad_cand, grad_out], axis=1)
            .reshape(row_count, gate_cols)
            .astype(bf16)
        )
        back_term = lax.dot_general(
            preact_grad, back_matrix, (((1,), (1,)), ((), ())), preferred_element_type=f32
        )
        next_hidden = (
            lax.psum_scatter(back_term, "mp", scatter_dimension=1, tiled=True) * keep_now[:, None]
        )
        next_cell = cell_grad * forget_gate * keep_now[:, None]
        return ((next_hidden, next_cell), preact_grad)

    zero_rows = jnp.zeros((row_count, local_units), f32)
    _, preact_grads = lax.scan(
        backward_step,
        (zero_rows, zero_rows),
        (preacts, cells, prev_cells, out_grads, keep_mask),
        reverse=True,
    )
    flat_prev = prevs.reshape(tokens_here, hidden_total)
    flat_pgrad = preact_grads.reshape(tokens_here, gate_cols)
    columns = flat_prev
    rec_grad = lax.psum_scatter(
        lax.dot_general(columns, flat_pgrad, (((0,), (0,)), ((), ())), preferred_element_type=f32),
        "dp",
        scatter_dimension=0,
        tiled=True,
    ).reshape(recurrent_weight.shape)
    onehot_ids = (
        time_ids.reshape(tokens_here)[:, None] == jnp.arange(vocab_size, dtype=jnp.int32)[None, :]
    ).astype(bf16)
    table_part = lax.dot_general(
        onehot_ids, flat_pgrad, (((0,), (0,)), ((), ())), preferred_element_type=f32
    )
    table_sum, dec_bias_grad, loss_data = lax.psum((table_part, dec_bias_part, loss_part), "dp")
    in_grad = jnp.dot(embedding.astype(f32).T, table_sum, precision=highest).reshape(
        width_in, 4, local_units
    )
    bias_grad = jnp.sum(table_sum, axis=0).reshape(4, local_units)
    emb_part = lax.dot_general(
        table_sum,
        input_weight.reshape(width_in, gate_cols).astype(f32),
        (((1,), (1,)), ((), ())),
        precision=highest,
    )
    emb_grad, loss = lax.psum((emb_part, loss_data), "mp")
    return (loss, emb_grad, in_grad, rec_grad, bias_grad, dec_grad, dec_bias_grad)


def solution(mesh):
    in_specs = (
        P("dp", None),
        P("dp", None),
        P("dp", None),
        P(),
        P(None, None, "mp"),
        P("dp", None, "mp"),
        P(None, "mp"),
        P("mp", "dp", None, None),
        P(),
    )
    out_specs = (
        P(),
        P(),
        P(None, None, "mp"),
        P("dp", None, "mp"),
        P(None, "mp"),
        P("mp", "dp", None, None),
        P(),
    )
    return jax.shard_map(
        on_device, mesh=mesh, in_specs=in_specs, out_specs=out_specs, check_vma=False
    )
```

profile of v0, /device:TPU:1, one launch (start us, length us, event | category | flops | bytes accessed | tf_op | source)
XLA Modules:
  0.0 1043.3 jit_solution(15943818408358508624)
XLA Ops:
  11.2 4.9 gather_fusion
  16.1 27.6 %all_gather.11 = bf16[1,8,64,275]{3,2,0,1:T(8,128)(2,1)S(1)} all-gather(bf16[1,1,64,275]{3,2,0,1:T(8,128)(2,1)S(1)} %bitcast.215), channel_id=1, replica_groups=mesh['dp'=8,'mp'=4] {'dp'}, dimensions={1}, use_global_device_ids=true | all-gather | bytes 316800 | tf_op jit(solution)/shard_map/all_gather | solution.py:30
  43.8 6.0 select_add_fusion
  49.8 90.0 %all-gather.2.cloned.1.call-done = bf16[2048,4,512]{2,1,0:T(4,128)(2,1)} async-done(((bf16[256,4,512]{2,1,0:T(4,128)(2,1)}), bf16[2048,4,512]{2,1,0:T(4,128)(2,1)}) %all-gather.2.cloned.1.call-update) | async-done | bytes 8388624 | tf_op jit(solution)/shard_map/all_gather | solution.py:29
  139.8 10.2 copy.89
  150.1 105.5 %while.40 = (s32[]{:T(128)}, bf16[128,512]{1,0:T(8,128)(2,1)S(1)}, f32[128,512]{1,0:T(8,128)S(1)}, bf16[6,128,2048]{2,1,0:T(8,128)(2,1)}, f32[6,128,2048]{2,1,0:...) while((s32[]{:T(128)}, bf16[128,512]{1,0:T(8,128)(2,1)S(1)}, ...), condition=%wide.region_1.2_spmd.clone, body=%wide.region_0.1_spmd.clone.sunk | while | flops 1076428928 | bytes 20582788 | solution.py:61
  150.1 8.1 all_gather.14
  158.2 6.0 bitcast_dynamic-update-slice_fusion.8
  168.3 7.3 all_gather.14
  175.6 6.0 bitcast_dynamic-update-slice_fusion.8
  185.8 7.3 all_gather.14
  193.1 6.1 bitcast_dynamic-update-slice_fusion.8
  203.3 7.3 all_gather.14
  210.6 6.0 bitcast_dynamic-update-slice_fusion.8
  220.7 7.3 all_gather.14
  228.0 6.0 bitcast_dynamic-update-slice_fusion.8
  238.1 7.3 all_gather.14
  245.4 6.0 bitcast_dynamic-update-slice_fusion.8
  255.6 2.5 fusion.50
  258.1 1.4 slice.51
  259.5 1.4 pad_multiply_fusion
  260.9 28.8 %all-reduce.6.cloned.1.call-done = f32[768,275]{0,1:T(8,128)} async-done(((f32[768,275]{0,1:T(8,128)}), f32[768,275]{0,1:T(8,128)}) %all-reduce.6.cloned.1.call-update) | async-done | bytes 844816 | tf_op jit(solution)/shard_map/psum | solution.py:67
  291.0 1.5 select_reduce_fusion
  293.1 1.6 convert_reduce_fusion
  295.2 1.8 fusion.38
  296.9 2.1 broadcast.51
  299.1 235.1 %while.41 = (s32[]{:T(128)}, f32[128,512]{1,0:T(8,128)S(1)}, f32[128,512]{1,0:T(8,128)S(1)}, bf16[6,128,2048]{1,2,0:T(8,128)(2,1)}, f32[6,128,512]{2,1,0:T(8,128...) while((s32[]{:T(128)}, f32[128,512]{1,0:T(8,128)S(1)}, ...), condition=%wide.region_11.12_spmd.clone, body=%wide.region_9.11_spmd.clone.sunk | while | flops 1077673984 | bytes 30935248 | solution.py:127
  302.6 1.5 fusion.88
  304.5 7.3 fusion.89
  312.7 25.5 %reduce-scatter.8.cloned.1.call-done = f32[128,512]{1,0:T(8,128)} async-done(((f32[128,2048]{1,0:T(8,128)}), f32[128,512]{1,0:T(8,128)}) %reduce-scatter.8.cloned.1.call-update) | async-done | bytes 262160 | tf_op jit(solution)/shard_map/while/body/eval_jaxpr/reduce_scatter | solution.py:121
  339.3 1.3 constant_dynamic-slice_fusion.4
  342.9 1.5 fusion.88
  344.8 7.3 fusion.89
  353.0 24.2 %reduce-scatter.8.cloned.1.call-done = f32[128,512]{1,0:T(8,128)} async-done(((f32[128,2048]{1,0:T(8,128)}), f32[128,512]{1,0:T(8,128)}) %reduce-scatter.8.cloned.1.call-update) | async-done | bytes 262160 | tf_op jit(solution)/shard_map/while/body/eval_jaxpr/reduce_scatter | solution.py:121
  378.3 1.3 constant_dynamic-slice_fusion.4
  381.9 1.5 fusion.88
  383.8 7.3 fusion.89
  392.0 24.2 %reduce-scatter.8.cloned.1.call-done = f32[128,512]{1,0:T(8,128)} async-done(((f32[128,2048]{1,0:T(8,128)}), f32[128,512]{1,0:T(8,128)}) %reduce-scatter.8.cloned.1.call-update) | async-done | bytes 262160 | tf_op jit(solution)/shard_map/while/body/eval_jaxpr/reduce_scatter | solution.py:121
  417.3 1.3 constant_dynamic-slice_fusion.4
  420.9 1.5 fusion.88
  422.7 7.3 fusion.89
  430.9 24.2 %reduce-scatter.8.cloned.1.call-done = f32[128,512]{1,0:T(8,128)} async-done(((f32[128,2048]{1,0:T(8,128)}), f32[128,512]{1,0:T(8,128)}) %reduce-scatter.8.cloned.1.call-update) | async-done | bytes 262160 | tf_op jit(solution)/shard_map/while/body/eval_jaxpr/reduce_scatter | solution.py:121
  456.3 1.3 constant_dynamic-slice_fusion.4
  459.8 1.5 fusion.88
  461.7 7.3 fusion.89
  469.9 24.2 %reduce-scatter.8.cloned.1.call-done = f32[128,512]{1,0:T(8,128)} async-done(((f32[128,2048]{1,0:T(8,128)}), f32[128,512]{1,0:T(8,128)}) %reduce-scatter.8.cloned.1.call-update) | async-done | bytes 262160 | tf_op jit(solution)/shard_map/while/body/eval_jaxpr/reduce_scatter | solution.py:121
  498.8 1.5 fusion.88
  500.7 7.4 fusion.89
  508.9 24.2 %reduce-scatter.8.cloned.1.call-done = f32[128,512]{1,0:T(8,128)} async-done(((f32[128,2048]{1,0:T(8,128)}), f32[128,512]{1,0:T(8,128)}) %reduce-scatter.8.cloned.1.call-update) | async-done | bytes 262160 | tf_op jit(solution)/shard_map/while/body/eval_jaxpr/reduce_scatter | solution.py:121
  534.2 4.8 copy.71
  539.0 4.6 fusion.36
  543.7 12.4 %convolution_bitcast_fusion = f32[2048,2048]{1,0:T(8,128)} fusion(bf16[6,128,2048]{2,1,0:T(8,128)(2,1)} %get-tuple-element.264, bf16[6,128,2048]{1,2,0:T(8,128)(2,1)S(1)} %copy-done.2), kind=kOutput, calls=%fused_computation.71 | convolution fusion | flops 6442450944 | bytes 23068672 | tf_op jit(solution)/shard_map/dot_general | solution.py:137
  557.3 1.5 fusion.52
  559.5 19.5 %all-reduce.1 = (f32[]{:T(128)}, f32[275]{0:T(512)}) all-reduce(f32[]{:T(128)S(6)} %select_n.15, f32[275]{0:T(512)S(1)} %get-tuple-element.442), channel_id=1, replica_groups=mesh['dp'=8,'mp'=4] {'dp'}, use_global_device_ids=true, to_apply=%region_7.8 | all-reduce | flops 276 | bytes 2208 | tf_op jit(solution)/shard_map/psum | solution.py:148
  579.0 9.4 psum.44
  588.4 62.2 %all-reduce.8.cloned.1.call-done = f32[275,2048]{1,0:T(8,128)} async-done(((f32[275,2048]{1,0:T(8,128)}), f32[275,2048]{1,0:T(8,128)}) %all-reduce.8.cloned.1.call-update) | async-done | bytes 2252816 | tf_op jit(solution)/shard_map/psum | solution.py:148
  650.6 3.6 fusion.51
  654.2 1.4 convolution_bitcast_fusion.1
  655.6 1.4 reshape.156
  657.8 279.7 %reduce-scatter.4.cloned.1.call-done = f32[256,2048]{1,0:T(8,128)} async-done(((f32[2048,2048]{1,0:T(8,128)}), f32[256,2048]{1,0:T(8,128)}) %reduce-scatter.4.cloned.1.call-update) | async-done | bytes 2097168 | tf_op jit(solution)/shard_map/reduce_scatter | solution.py:136
  937.4 3.6 reshape.157
  941.1 60.0 %reduce-scatter.6.cloned.1.call-done = f32[64,275]{1,0:T(8,128)} async-done(((f32[512,275]{1,0:T(8,128)}), f32[64,275]{1,0:T(8,128)}) %reduce-scatter.6.cloned.1.call-update) | async-done | bytes 70416 | tf_op jit(solution)/shard_map/reduce_scatter | solution.py:83
  1001.1 33.8 %all-reduce.10.cloned.1.call-done = f32[275,100]{1,0:T(8,128)} async-done(((f32[275,100]{1,0:T(8,128)}), f32[275,100]{1,0:T(8,128)}) %all-reduce.10.cloned.1.call-update) | async-done | bytes 110016 | tf_op jit(solution)/shard_map/psum | solution.py:159
  1034.8 1.6 copy.193
  (187 shorter events, 62.7 us)
Async XLA Ops:
  7.2 3.6 copy-start
  7.2 132.7 %all-gather.2.cloned.1.call-start = ((), (), s32[]{:S(2)}) async-start(), calls=%async_computation.3 | async-start | bytes 9437184 | tf_op jit(solution)/shard_map/all_gather | solution.py:29
  7.9 281.7 %all-reduce.6.cloned.1.call-start = ((), (), s32[]{:S(2)}) async-start(), calls=%async_computation.4 | async-start | bytes 1720320 | tf_op jit(solution)/shard_map/psum | solution.py:67
  9.3 6.9 copy-start.5
  11.2 5.0 copy-start.8
  11.2 32.6 %copy-start.9 = (s32[128,6]{0,1:T(8,128)S(1)}, s32[128,6]{0,1:T(8,128)}, u32[]{:S(2)}) copy-start(s32[128,6]{0,1:T(8,128)} %param.13) | copy-start | bytes 9220
  11.2 32.6 %copy-start.12 = (s32[128,6]{0,1:T(8,128)S(1)}, s32[128,6]{0,1:T(8,128)}, u32[]{:S(2)}) copy-start(s32[128,6]{0,1:T(8,128)} %param.15) | copy-start | bytes 9220
  258.0 31.6 %copy-start.10 = (f32[275]{0:T(512)S(1)}, f32[275]{0:T(512)}, u32[]{:S(2)}) copy-start(f32[275]{0:T(512)} %param.21) | copy-start | bytes 3304
  258.1 32.9 %copy-start.11 = (s32[128,6]{0,1:T(8,128)S(1)}, s32[128,6]{0,1:T(8,128)}, u32[]{:S(2)}) copy-start(s32[128,6]{0,1:T(8,128)} %param.14) | copy-start | bytes 9220
  294.7 4.4 copy-start.3
  299.1 39.2 %reduce-scatter.8.cloned.1.call-start = ((), (), s32[]{:S(2)}) async-start(), calls=%async_computation.9 | async-start | bytes 1310720 | tf_op jit(solution)/shard_map/while/body/eval_jaxpr/reduce_scatter | solution.py:121
  339.3 37.9 %reduce-scatter.8.cloned.1.call-start = ((), (), s32[]{:S(2)}) async-start(), calls=%async_computation.9 | async-start | bytes 1310720 | tf_op jit(solution)/shard_map/while/body/eval_jaxpr/reduce_scatter | solution.py:121
  378.3 37.9 %reduce-scatter.8.cloned.1.call-start = ((), (), s32[]{:S(2)}) async-start(), calls=%async_computation.9 | async-start | bytes 1310720 | tf_op jit(solution)/shard_map/while/body/eval_jaxpr/reduce_scatter | solution.py:121
  417.2 37.9 %reduce-scatter.8.cloned.1.call-start = ((), (), s32[]{:S(2)}) async-start(), calls=%async_computation.9 | async-start | bytes 1310720 | tf_op jit(solution)/shard_map/while/body/eval_jaxpr/reduce_scatter | solution.py:121
  456.2 37.9 %reduce-scatter.8.cloned.1.call-start = ((), (), s32[]{:S(2)}) async-start(), calls=%async_computation.9 | async-start | bytes 1310720 | tf_op jit(solution)/shard_map/while/body/eval_jaxpr/reduce_scatter | solution.py:121
  495.2 37.9 %reduce-scatter.8.cloned.1.call-start = ((), (), s32[]{:S(2)}) async-start(), calls=%async_computation.9 | async-start | bytes 1310720 | tf_op jit(solution)/shard_map/while/body/eval_jaxpr/reduce_scatter | solution.py:121
  534.1 116.4 %all-reduce.8.cloned.1.call-start = ((), (), s32[]{:S(2)}) async-start(), calls=%async_computation.5 | async-start | bytes 4587520 | tf_op jit(solution)/shard_map/psum | solution.py:148
  539.0 4.7 copy-start.2
  543.6 393.9 %reduce-scatter.4.cloned.1.call-start = ((), (), s32[]{:S(2)}) async-start(), calls=%async_computation.7 | async-start | bytes 18874368 | tf_op jit(solution)/shard_map/reduce_scatter | solution.py:136
  556.0 1.0 copy-start.4
  556.0 1.3 copy-start.7
  556.0 94.5 %copy-start.6 = (bf16[13,8,4,512]{3,1,2,0:T(8,128)(2,1)S(1)}, bf16[13,8,4,512]{3,1,2,0:T(8,128)(2,1)}, u32[]{:S(2)}) copy-start(bf16[13,8,4,512]{3,1,2,0:T(8,128)(2,1)} %copy-done.5) | copy-start | bytes 1277956
  556.0 445.0 %reduce-scatter.6.cloned.1.call-start = ((), (), s32[]{:S(2)}) async-start(), calls=%async_computation.8 | async-start | bytes 884736 | tf_op jit(solution)/shard_map/reduce_scatter | solution.py:83
  558.8 476.0 %all-reduce.10.cloned.1.call-start = ((), (), s32[]{:S(2)}) async-start(), calls=%async_computation.6 | async-start | bytes 286720 | tf_op jit(solution)/shard_map/psum | solution.py:159
  650.6 3.6 copy-start.1
Sparse Core Ops, SparseCore 0:
  10.1 129.6 all-gather.1
  258.2 31.4 all-reduce.5
  312.0 26.1 reduce-scatter.7
  352.3 24.9 reduce-scatter.7
  391.3 24.8 reduce-scatter.7
  430.2 24.8 reduce-scatter.7
  469.2 24.8 reduce-scatter.7
  508.2 24.8 reduce-scatter.7
  543.7 106.7 all-reduce.7
  654.7 282.7 reduce-scatter.3
  941.3 59.6 reduce-scatter.5
  1003.9 30.8 all-reduce.9
where the time goes:
time: 1050 us; the launch traced here: 1040 us
  waiting for transfers between devices  702 us (67%)
  matrix products  108 us (10%)
  blocking collectives  101 us (10%)
  local copies, waits for them, and re-layouts  67.6 us (6%)
  other arithmetic  48.2 us (5%)
  between operations  15 us (1%)
    reduce_scatter x1, waiting for transfers between devices, on_device(): lax.psum_scatter(lax.dot_general(columns, flat_pgrad, (((0,), (0,)), ((),...  280 us
    reduce_scatter x6, waiting for transfers between devices, backward_step(): lax.psum_scatter(back_term, 'mp', scatter_dimension=1, tiled=True)  147 us
    all_gather x1, waiting for transfers between devices, on_device(): lax.all_gather(recurrent_weight, 'dp', axis=0, tiled=True)  90 us
    psum x1, waiting for transfers between devices, on_device(): lax.psum((table_part, dec_bias_part, loss_part), 'dp')  62.2 us
    reduce_scatter x1, waiting for transfers between devices, on_device(): lax.psum_scatter(lax.dot_general(columns, grad_rows, (((0,), (0,)), ((),...  60 us
    all_gather x6, blocking collectives, forward_step(): hidden_full = lax.all_gather(hidden_loc, 'mp', axis=1, tiled=True)  44.5 us
    dot_general x6, matrix products, backward_step(): lax.dot_general(preact_grad, back_matrix, (((1,), (1,)), ((), ())), prefe...  44.1 us
    dot_general x6, matrix products, forward_step(): jnp.dot(previous, rec_matrix, preferred_element_type=f32)  36.1 us
  transfers between devices with their start and end apart: 12, of which 12 were waited for; matrix products, arithmetic and copies ran while one was open for 4% of the time, Pallas kernels for 0%

commit v1 on v0

--- a/solution.py
+++ b/solution.py
@@ -1,7 +1,823 @@
+import functools
+
 import jax
 import jax.numpy as jnp
 from jax import lax
+from jax.experimental import pallas as pl
+from jax.experimental.pallas import tpu as pltpu
 from jax.sharding import PartitionSpec as P
+
+f32 = jnp.float32
+bf16 = jnp.bfloat16
+MESH = pl.DeviceIdType.MESH
+LANES = 128
+CHIPS = ((2, 0), (0, 2), (2, 2))
+PEERS = ((0, 1), (2, 0), (0, 2), (2, 2), (2, 1), (0, 3), (2, 3), (1, 0), (4, 0), (5, 0), (6, 0))
+GROUP = ((0, 1), (2, 0), (0, 2), (2, 2), (2, 1), (0, 3), (2, 3))
+OTHERS = (1, 4, 5)
+COLUMN = (4, 6, 2)
+SPLIT = 2
+PIECES = 4
+
+
+def turn(value, flips):
+    for bit in (1, 2, 4):
+        if flips & bit:
+            value = value + bit - 2 * bit * lax.rem(lax.div(value, bit), 2)
+    return value
+
+
+def dot(a, b):
+    return jnp.dot(a, b, preferred_element_type=f32)
+
+
+def dot_t(a, b):
+    return lax.dot_general(a, b, (((1,), (1,)), ((), ())), preferred_element_type=f32)
+
+
+def t_dot(a, b):
+    return lax.dot_general(a, b, (((0,), (0,)), ((), ())), preferred_element_type=f32)
+
+
+def layer_kernel(
+    dims,
+    ids_ref,
+    rec_ref,
+    emb_ref,
+    iw_ref,
+    gb_ref,
+    dec_ref,
+    decb_ref,
+    out_rec,
+    out_iw,
+    out_emb,
+    out_dec,
+    out_small,
+    ids_all,
+    weights,
+    dec_all,
+    hid,
+    gates,
+    cells,
+    onehots,
+    embedded,
+    keeps,
+    targets,
+    logit_grads,
+    pgs,
+    pgm,
+    carry_c,
+    own_part,
+    own_sum,
+    core_out,
+    core_in,
+    chip_out,
+    chip_in,
+    small_acc,
+    both,
+    acc,
+    x_out,
+    x_in,
+    z_out,
+    z_in,
+    giw_acc,
+    giw_out,
+    giw_x_in,
+    giw_z_out,
+    giw_z_in,
+    giw_full,
+    emb_part,
+    emb_in,
+    emb_sums,
+    emb_full,
+    dec_part,
+    dec_in,
+    small_all,
+    ids_sem,
+    wz_sem,
+    wx_sem,
+    decg_sem,
+    decr_sem,
+    hid_sem,
+    relay_sem,
+    core_sem,
+    chip_sem,
+    gx_sem,
+    gz_sem,
+    giw_sem,
+    emb_sem,
+    emb2_sem,
+    emb3_sem,
+    dsum_sem,
+    small_sem,
+):
+    steps, rows, units, vocab_pad, tokens_all, block = dims
+    cols = 4 * units
+    part = rows // SPLIT
+    d, m = lax.axis_index("dp"), lax.axis_index("mp")
+    x_at, z_low, z_high = lax.rem(d, 2), lax.rem(lax.div(d, 2), 2), lax.div(d, 4)
+    z_at = lax.div(d, 2)
+
+    def device(flips):
+        return (turn(d, flips[0]), turn(m, flips[1]))
+
+    def slot(flips):
+        return turn(m, flips[1]) * 2 + turn(z_low, flips[0] // 2)
+
+    own = slot((0, 0))
+
+    def copy(src, dst, sems, at, flips):
+        return pltpu.make_async_remote_copy(
+            src_ref=src,
+            dst_ref=dst,
+            send_sem=sems.at[(0,) + at],
+            recv_sem=sems.at[(1,) + at],
+            device_id=device(flips),
+            device_id_type=MESH,
+        )
+
+    barrier = pltpu.get_barrier_semaphore()
+    for flips in PEERS:
+        pl.semaphore_signal(barrier, inc=1, device_id=device(flips), device_id_type=MESH)
+    pl.semaphore_wait(barrier, len(PEERS))
+
+    piece = block // PIECES
+
+    def weight_rows(index, p):
+        first = p * piece
+        side, inside = first // LANES, first % LANES
+        return weights.at[
+            lax.div(index, 2) * 2 + side,
+            pl.ds(pl.multiple_of(lax.rem(index, 2) * LANES + inside, piece), piece),
+        ]
+
+    def weight_z(k, p):
+        flips = COLUMN[k]
+        half = turn(z_low, (flips & 2) // 2)
+        return copy(
+            rec_ref.at[half, pl.ds(p * piece, piece)], weight_rows(d, p), wz_sem, (k, p), (flips, 0)
+        )
+
+    def weight_z_in(k, p):
+        spot = weight_rows(turn(d, COLUMN[k]), p)
+        return copy(spot, spot, wz_sem, (k, p), (COLUMN[k], 0))
+
+    def weight_x(k, p):
+        if k == 3:
+            return copy(
+                rec_ref.at[z_low, pl.ds(p * piece, piece)],
+                weight_rows(d, p),
+                wx_sem,
+                (k, p),
+                (1, 0),
+            )
+        spot = weight_rows(turn(d, COLUMN[k]), p)
+        return copy(spot, spot, wx_sem, (k, p), (1, 0))
+
+    def weight_x_in(k, p):
+        flips = 0 if k == 3 else COLUMN[k]
+        spot = weight_rows(turn(d, flips + 1), p)
+        return copy(spot, spot, wx_sem, (k, p), (1, 0))
+
+    ids_copy = copy(ids_ref, ids_all.at[z_low], ids_sem, (0,), (2, 0))
+    ids_copy.start()
+    dec_rows = dec_ref.shape[0]
+    dec_spot = dec_all.at[
+        own, pl.ds(pl.multiple_of(z_high * LANES + x_at * dec_rows, dec_rows), dec_rows)
+    ]
+    dec_copies = [
+        copy(dec_ref, dec_spot, decg_sem, (j,), (flips, 0)) for j, flips in enumerate(OTHERS)
+    ]
+    for each in dec_copies:
+        each.start()
+    for p in range(PIECES):
+        for k in range(3):
+            weight_z(k, p).start()
+        weight_x(3, p).start()
+
+    ids_all[z_low] = ids_ref[...]
+    dec_spot[...] = dec_ref[...]
+    for p in range(PIECES):
+        weight_rows(d, p)[...] = rec_ref[z_low, pl.ds(p * piece, piece), :]
+    ids_copy.wait_recv()
+    ids_now = ids_all[...].reshape(rows, LANES)
+    vocab_iota = lax.broadcasted_iota(jnp.int32, (rows, vocab_pad), 1)
+    for t in range(steps):
+        onehots[t] = (ids_now[:, t : t + 1] == vocab_iota).astype(f32).astype(bf16)
+        targets[t] = jnp.broadcast_to(ids_now[:, steps + t : steps + t + 1], (rows, LANES))
+        keeps[t] = jnp.broadcast_to(
+            (1 - ids_now[:, 2 * steps + t : 2 * steps + t + 1]).astype(f32), (rows, LANES)
+        )
+
+    def project(t, _):
+        chosen = dot(onehots[t], emb_ref[...]).astype(bf16)
+        embedded[t] = chosen
+        gates[t] = dot(chosen, iw_ref[z_low]) + gb_ref[z_low]
+        return 0
+
+    lax.fori_loop(0, steps, project, 0)
+
+    def span(s):
+        return pl.ds(s * part, part)
+
+    def send_hidden(t, s):
+        spot = hid.at[own, t, span(s)]
+        for j, flips in enumerate(CHIPS + ((0, 1),)):
+            copy(spot, spot, hid_sem, (t, s, j), flips).start()
+
+    def hidden_in(t, s, j):
+        flips = CHIPS[j] if j < 3 else (0, 1)
+        spot = hid.at[slot(flips), t, span(s)]
+        return copy(spot, spot, hid_sem, (t, s, j), flips)
+
+    def hidden_relay(t, s, j):
+        spot = hid.at[slot(CHIPS[j]), t, span(s)]
+        return copy(spot, spot, relay_sem, (t, s, j), (0, 1))
+
+    def relay_in(t, s, j):
+        spot = hid.at[slot((CHIPS[j][0], CHIPS[j][1] + 1)), t, span(s)]
+        return copy(spot, spot, relay_sem, (t, s, j), (0, 1))
+
+    def relay(t, s):
+        for j in range(3):
+            hidden_in(t, s, j).wait_recv()
+            hidden_relay(t, s, j).start()
+
+    def cell_step(t, s, added):
+        here = span(s)
+        preact = gates[t, here]
+        if added is not None:
+            keep = keeps[t, here, :1]
+            preact = preact + keep * added
+        in_gate = jax.nn.sigmoid(preact[:, :units])
+        forget = jax.nn.sigmoid(preact[:, units : 2 * units])
+        candidate = jnp.tanh(preact[:, 2 * units : 3 * units])
+        out_gate = jax.nn.sigmoid(preact[:, 3 * units :])
+        cell = in_gate * candidate
+        if added is not None:
+            cell = forget * keep * cells[t - 1, here] + cell
+        cells[t, here] = cell
+        hid[own, t, here] = (out_gate * jnp.tanh(cell)).astype(bf16)
+        send_hidden(t, s)
+        gates[t, here, :units] = in_gate
+        gates[t, here, units : 2 * units] = forget
+        gates[t, here, 2 * units : 3 * units] = candidate
+        gates[t, here, 3 * units :] = out_gate
+
+    for s in range(SPLIT):
+        cell_step(0, s, None)
+
+    for j, flips in enumerate(OTHERS):
+        at = turn(z_high, flips // 4) * LANES + turn(x_at, flips % 2) * dec_rows
+        spot = dec_all.at[own, pl.ds(pl.multiple_of(at, dec_rows), dec_rows)]
+        copy(spot, spot, decg_sem, (j,), (flips, 0)).wait_recv()
+    dec_own = dec_all.at[own]
+    dec_sends = [
+        copy(dec_own, dec_own, decr_sem, (j,), flips) for j, flips in enumerate(CHIPS + ((0, 1),))
+    ]
+    for each in dec_sends:
+        each.start()
+
+    def passing(p):
+        for k in range(3):
+            weight_z_in(k, p).wait_recv()
+            weight_x(k, p).start()
+
+    passing(0)
+    for s in range(SPLIT):
+        relay(0, s)
+    passing(1)
+    dec_relays = []
+    for j in range(3):
+        spot = dec_all.at[slot(CHIPS[j])]
+        copy(spot, spot, decr_sem, (j,), CHIPS[j]).wait_recv()
+        each = copy(spot, spot, decr_sem, (4 + j,), (0, 1))
+        each.start()
+        dec_relays.append(each)
+    for p in range(2, PIECES):
+        passing(p)
+    spot = dec_all.at[slot((0, 1))]
+    copy(spot, spot, decr_sem, (3,), (0, 1)).wait_recv()
+    for j in range(3):
+        spot = dec_all.at[slot((CHIPS[j][0], CHIPS[j][1] + 1))]
+        copy(spot, spot, decr_sem, (4 + j,), (0, 1)).wait_recv()
+    for p in range(PIECES):
+        for k in (3, 0, 1, 2):
+            weight_x_in(k, p).wait_recv()
+
+    def add_member(total, t, s, flips):
+        at = slot(flips)
+        more = dot(hid[at, t, span(s)], weights[at])
+        return more if total is None else total + more
+
+    def gather_hidden(t, s):
+        relay(t, s)
+        total = add_member(None, t, s, (0, 0))
+        for j in range(3):
+            total = add_member(total, t, s, CHIPS[j])
+        return finish_hidden(t, s, total)
+
+    def finish_hidden(t, s, total):
+        hidden_in(t, s, 3).wait_recv()
+        total = add_member(total, t, s, (0, 1))
+        for j in range(3):
+            relay_in(t, s, j).wait_recv()
+            total = add_member(total, t, s, (CHIPS[j][0], CHIPS[j][1] + 1))
+        return total
+
+    vocab_part = lax.broadcasted_iota(jnp.int32, (part, vocab_pad), 1)
+    small_acc[...] = jnp.zeros_like(small_acc)
+
+    def decode(t, s):
+        here = span(s)
+        logits = decb_ref[...]
+        for at in range(8):
+            logits = logits + dot(hid[at, t, here], dec_all[at])
+        top = jnp.max(logits, axis=1, keepdims=True)
+        exps = jnp.exp(logits - top)
+        total = jnp.sum(exps, axis=1, keepdims=True)
+        hot = targets[t, here, :1] == vocab_part
+        picked = jnp.sum(jnp.where(hot, logits, 0.0), axis=1, keepdims=True)
+        lost = top + jnp.log(total) - picked
+        grad = ((exps / total - jnp.where(hot, 1.0, 0.0)) / tokens_all).astype(bf16)
+        logit_grads[t, here] = grad
+        small_acc[0:1, :] += jnp.sum(grad.astype(f32), axis=0, keepdims=True)
+        small_acc[1:2, :] += jnp.broadcast_to(
+            jnp.sum(lost, axis=0, keepdims=True) / tokens_all, (1, vocab_pad)
+        )
+
+    def forward(t, _):
+        for s in range(SPLIT):
+            cell_step(t, s, gather_hidden(t - 1, s))
+            decode(t - 1, s)
+        return 0
+
+    for s in range(SPLIT):
+        total = None
+        for flips in ((0, 0),) + CHIPS:
+            total = add_member(total, 0, s, flips)
+        cell_step(1, s, finish_hidden(0, s, total))
+        decode(0, s)
+    lax.fori_loop(2, steps, forward, 0)
+
+    def cell_back(t, s, carried, first):
+        here = span(s)
+        hidden_grad = dot_t(logit_grads[t, here], dec_all[own])
+        if carried is not None:
+            hidden_grad = hidden_grad + carried
+        in_gate = gates[t, here, :units]
+        forget = gates[t, here, units : 2 * units]
+        candidate = gates[t, here, 2 * units : 3 * units]
+        out_gate = gates[t, here, 3 * units :]
+        squash = jnp.tanh(cells[t, here])
+        cell_grad = hidden_grad * out_gate * (1.0 - squash * squash)
+        if carried is not None:
+            cell_grad = cell_grad + carry_c[here]
+        grads = [
+            cell_grad * candidate * in_gate * (1.0 - in_gate),
+            None,
+            cell_grad * in_gate * (1.0 - candidate * candidate),
+            hidden_grad * squash * out_gate * (1.0 - out_gate),
+        ]
+        if first:
+            grads[1] = jnp.zeros_like(cell_grad)
+        else:
+            keep = keeps[t, here, :1]
+            grads[1] = cell_grad * (keep * cells[t - 1, here]) * forget * (1.0 - forget)
+            carry_c[here] = keep * forget * cell_grad
+        for k in range(4):
+            pgs[t, here, k * units : (k + 1) * units] = grads[k].astype(bf16)
+            if not first:
+                pgm[t - 1, here, k * units : (k + 1) * units] = (keep * grads[k]).astype(bf16)
+
+    def core_copy(t, s):
+        return copy(core_out.at[t - 1, s], core_in.at[t - 1, s], core_sem, (t - 1, s), (0, 1))
+
+    def chip_copy(t, s, j):
+        return copy(
+            chip_out.at[t - 1, s, j], chip_in.at[t - 1, s, j], chip_sem, (t - 1, s, j), CHIPS[j]
+        )
+
+    def spread(t, s):
+        here = span(s)
+        grad = pgm[t - 1, here]
+        chips = CHIPS + ((0, 0),)
+        for j, flips in enumerate(chips):
+            core_out[t - 1, s, j] = dot_t(grad, weights[slot((flips[0], flips[1] + 1))]).astype(bf16)
+        core_copy(t, s).start()
+        for j, flips in enumerate(chips):
+            own_part[j] = dot_t(grad, weights[slot(flips)])
+        core_copy(t, s).wait_recv()
+        for j in range(3):
+            chip_out[t - 1, s, j] = (own_part[j] + core_in[t - 1, s, j].astype(f32)).astype(bf16)
+            chip_copy(t, s, j).start()
+        own_sum[s] = own_part[3] + core_in[t - 1, s, 3].astype(f32)
+
+    def carried_in(t, s):
+        total = own_sum[s]
+        for j in range(3):
+            chip_copy(t + 1, s, j).wait_recv()
+            total = total + chip_in[t, s, j].astype(f32)
+        return total
+
+    last = steps - 1
+    for s in range(SPLIT):
+        relay(last, s)
+    for s in range(SPLIT):
+        hidden_in(last, s, 3).wait_recv()
+        for j in range(3):
+            relay_in(last, s, j).wait_recv()
+        decode(last, s)
+        cell_back(last, s, None, False)
+        spread(last, s)
+
+    def backward(i, _):
+        t = last - i
+        for s in range(SPLIT):
+            cell_back(t, s, carried_in(t, s), False)
+            spread(t, s)
+        return 0
+
+    lax.fori_loop(1, last, backward, 0)
+
+    far = (2, 3, 1, 0)
+
+    def x_copy(k, side):
+        return copy(x_out.at[k, side], x_in.at[k, side], gx_sem, (k, side), (1, 0))
+
+    def z_copy(k, side):
+        return copy(z_out.at[k, side], z_in.at[k, side], gz_sem, (k, side), (far[k] * 2, 0))
+
+    used = (steps - 1) * rows
+
+    def weight_grad(k):
+        block_z = turn(z_at, far[k])
+
+        def one(side, _):
+            at = block_z * 2 + side
+            both[...] = t_dot(
+                hid[at, 0 : steps - 1].reshape(used, units), pgm[...].reshape(used, cols)
+            ).reshape(2, LANES, cols)
+            x_out[k, side] = both[1 - x_at].astype(bf16)
+            x_copy(k, side).start()
+            acc[k, side] = both[x_at]
+            return 0
+
+        lax.fori_loop(0, 2, one, 0)
+
+    def pass_z(k, side):
+        x_copy(k, side).wait_recv()
+        total = acc[k, side] + x_in[k, side].astype(f32)
+        if k < 3:
+            z_out[k, side] = total.astype(bf16)
+            z_copy(k, side).start()
+        else:
+            acc[k, side] = total
+
+    weight_grad(0)
+    weight_grad(1)
+    weight_grad(2)
+    weight_grad(3)
+
+    for s in range(SPLIT):
+        cell_back(0, s, carried_in(0, s), True)
+    tokens = steps * rows
+    flat_grads = pgs[...].reshape(tokens, cols)
+    giw_rows = giw_acc.shape[0]
+    giw_acc[...] = t_dot(embedded[...].reshape(tokens, LANES), flat_grads)[:giw_rows]
+    for k in range(2):
+        at = pl.multiple_of((1 - x_at) * (2 * units) + k * units, units)
+        giw_out[k] = giw_acc[:, pl.ds(at, units)].astype(bf16)
+    giw_x = copy(giw_out, giw_x_in, giw_sem, (0,), (1, 0))
+    giw_x.start()
+
+    def dec_block(flips):
+        return turn(z_high, flips // 4) * 2 + turn(x_at, flips % 2)
+
+    dec_total = t_dot(hid[own].reshape(tokens, units), logit_grads[...].reshape(tokens, vocab_pad))
+    dec_part[...] = dec_total.reshape(4, dec_rows, vocab_pad)
+    dsum = [
+        copy(dec_part.at[dec_block(flips)], dec_in.at[dec_block(0)], dsum_sem, (j,), (flips, 0))
+        for j, flips in enumerate(OTHERS)
+    ]
+    for each in dsum:
+        each.start()
+    dec_in[dec_block(0)] = dec_part[dec_block(0)]
+    small_all[dec_block(0)] = small_acc[...]
+    smalls = [
+        copy(small_acc, small_all.at[dec_block(0)], small_sem, (j,), (flips, 0))
+        for j, flips in enumerate(OTHERS)
+    ]
+    for each in smalls:
+        each.start()
+
+    by_token = dot_t(flat_grads, iw_ref[z_low])
+    high = by_token.astype(bf16)
+    low = (by_token - high.astype(f32)).astype(bf16)
+    flat_hot = onehots[...].reshape(tokens, vocab_pad)
+    emb_rows = emb_full.shape[1]
+    emb_part[...] = (t_dot(flat_hot, high) + t_dot(flat_hot, low))[: 8 * emb_rows].reshape(
+        8, emb_rows, LANES
+    )
+    emb_copies = [
+        copy(emb_part.at[slot(flips)], emb_in.at[own], emb_sem, (j,), flips)
+        for j, flips in enumerate(GROUP)
+    ]
+    for each in emb_copies:
+        each.start()
+    emb_in[own] = emb_part[own]
+
+    pass_z(0, 0)
+
+    giw_x.wait_recv()
+    for k in range(2):
+        at = pl.multiple_of(x_at * (2 * units) + k * units, units)
+        giw_acc[:, pl.ds(at, units)] += giw_x_in[k].astype(f32)
+    giw_z_out[...] = giw_acc[
+        :, pl.ds(pl.multiple_of(x_at * (2 * units) + (1 - z_high) * units, units), units)
+    ].astype(bf16)
+    giw_z = copy(giw_z_out, giw_z_in, giw_sem, (1,), (4, 0))
+    giw_z.start()
+    pass_z(0, 1)
+    for j, flips in enumerate(GROUP):
+        copy(emb_part.at[own], emb_in.at[slot(flips)], emb_sem, (j,), flips).wait_recv()
+    total = emb_in[0]
+    for at in range(1, 8):
+        total = total + emb_in[at]
+    emb_sums[dec_block(0)] = total
+    emb2 = [
+        copy(
+            emb_sums.at[dec_block(0)], emb_sums.at[dec_block(0)], emb2_sem, (j,), (flips, 0)
+        )
+        for j, flips in enumerate(OTHERS)
+    ]
+    for each in emb2:
+        each.start()
+
+    giw_z.wait_recv()
+    gate_at = x_at * 2 + z_high
+    giw_full[z_low, gate_at] = (
+        giw_acc[:, pl.ds(pl.multiple_of(gate_at * units, units), units)] + giw_z_in[...].astype(f32)
+    ).astype(bf16)
+    spot = giw_full.at[z_low, gate_at]
+    giw_back_z = copy(spot, spot, giw_sem, (2,), (4, 0))
+    giw_back_z.start()
+    pass_z(1, 0)
+    for j, flips in enumerate(OTHERS):
+        spot = emb_sums.at[dec_block(flips)]
+        copy(spot, spot, emb2_sem, (j,), (flips, 0)).wait_recv()
+    emb_full[own] = (emb_sums[0] + emb_sums[1]) + (emb_sums[2] + emb_sums[3])
+    emb3 = [
+        copy(emb_full.at[own], emb_full.at[own], emb3_sem, (j,), flips)
+        for j, flips in enumerate(GROUP)
+    ]
+    for each in emb3:
+        each.start()
+    spot = giw_full.at[z_low, x_at * 2 + 1 - z_high]
+    copy(spot, spot, giw_sem, (2,), (4, 0)).wait_recv()
+    spot = giw_full.at[z_low, pl.ds(x_at * 2, 2)]
+    giw_back_x = copy(spot, spot, giw_sem, (3,), (1, 0))
+    giw_back_x.start()
+    pass_z(1, 1)
+    spot = giw_full.at[z_low, pl.ds((1 - x_at) * 2, 2)]
+    copy(spot, spot, giw_sem, (3,), (1, 0)).wait_recv()
+    spot = giw_full.at[z_low]
+    giw_side = copy(spot, spot, giw_sem, (4,), (2, 0))
+    giw_side.start()
+    for j, flips in enumerate(OTHERS):
+        copy(
+            dec_part.at[dec_block(0)], dec_in.at[dec_block(flips)], dsum_sem, (j,), (flips, 0)
+        ).wait_recv()
+        spot = small_all.at[dec_block(flips)]
+        copy(small_acc, spot, small_sem, (j,), (flips, 0)).wait_recv()
+    out_dec[...] = (dec_in[0] + dec_in[1]) + (dec_in[2] + dec_in[3])
+    out_small[...] = (small_all[0] + small_all[1]) + (small_all[2] + small_all[3])
+    pass_z(2, 0)
+    pass_z(2, 1)
+    for j, flips in enumerate(GROUP):
+        spot = emb_full.at[slot(flips)]
+        copy(spot, spot, emb3_sem, (j,), flips).wait_recv()
+    out_emb[...] = emb_full[...]
+    spot = giw_full.at[1 - z_low]
+    copy(spot, spot, giw_sem, (4,), (2, 0)).wait_recv()
+    runs = units // LANES
+
+    def scatter(ref, here, side, gate, value):
+        for run in range(runs):
+            at = pl.multiple_of(gate * 2 * units + run * 2 * LANES + side * LANES, LANES)
+            ref[here, pl.ds(at, LANES)] = value[:, run * LANES : (run + 1) * LANES]
+
+    for side in range(2):
+        for gate in range(4):
+            scatter(out_iw, slice(None), side, gate, giw_full[side, gate].astype(f32))
+    pass_z(3, 0)
+    pass_z(3, 1)
+    for side in range(2):
+        here = pl.ds(side * LANES, LANES)
+        z_copy(0, side).wait_recv()
+        for gate in range(4):
+            mine = slice(gate * units, (gate + 1) * units)
+            scatter(
+                out_rec,
+                here,
+                z_low,
+                gate,
+                acc[3, side, :, mine] + z_in[0, side, :, mine].astype(f32),
+            )
+        z_copy(1, side).wait_recv()
+        z_copy(2, side).wait_recv()
+        for gate in range(4):
+            mine = slice(gate * units, (gate + 1) * units)
+            scatter(
+                out_rec,
+                here,
+                1 - z_low,
+                gate,
+                z_in[1, side, :, mine].astype(f32) + z_in[2, side, :, mine].astype(f32),
+            )
+
+    ids_copy.wait_send()
+    for each in dec_copies + dec_sends + dec_relays:
+        each.wait_send()
+    for p in range(PIECES):
+        for k in range(3):
+            weight_z(k, p).wait_send()
+        for k in range(4):
+            weight_x(k, p).wait_send()
+
+    def sent(t, _):
+        for s in range(SPLIT):
+            for j in range(3):
+                hidden_in(t, s, j).wait_send()
+                hidden_relay(t, s, j).wait_send()
+            hidden_in(t, s, 3).wait_send()
+        return 0
+
+    lax.fori_loop(0, steps, sent, 0)
+
+    def sent_back(t, _):
+        for s in range(SPLIT):
+            core_copy(t, s).wait_send()
+            for j in range(3):
+                chip_copy(t, s, j).wait_send()
+        return 0
+
+    lax.fori_loop(1, steps, sent_back, 0)
+    for side in range(2):
+        for k in range(4):
+            x_copy(k, side).wait_send()
+        for k in range(3):
+            z_copy(k, side).wait_send()
+    for each in [giw_x, giw_z, giw_back_z, giw_back_x, giw_side]:
+        each.wait_send()
+    for each in emb_copies + emb2 + emb3 + dsum + smalls:
+        each.wait_send()
+
+
+def grouped(
+    char_ids,
+    next_chars,
+    resets,
+    embedding,
+    input_weight,
+    recurrent_weight,
+    gate_bias,
+    decoder_weight,
+    decoder_bias,
+):
+    data_count = lax.axis_size("dp")
+    row_count, steps = char_ids.shape
+    vocab, width = embedding.shape
+    local_units = input_weight.shape[2]
+    block = recurrent_weight.shape[0]
+    units = local_units // 2
+    cols = 4 * units
+    runs = units // LANES
+    rows = 2 * row_count
+    dec_rows = decoder_weight.shape[2]
+    vocab_pad = pl.cdiv(vocab, LANES) * LANES
+    tokens_all = row_count * steps * data_count
+    part = rows // SPLIT
+    emb_rows = pl.cdiv(vocab, 64) * 8
+    giw_rows = pl.cdiv(width + 1, 16) * 16
+
+    ids = jnp.pad(
+        jnp.concatenate([char_ids, next_chars, resets], axis=1), ((0, 0), (0, LANES - 3 * steps))
+    )
+    rec = (
+        recurrent_weight.reshape(block, 4, runs, 2, LANES)
+        .transpose(3, 0, 1, 2, 4)
+        .reshape(2, block, cols)
+    )
+    emb = jnp.concatenate([embedding, jnp.ones((vocab, 1), bf16)], axis=1)
+    emb = jnp.pad(emb, ((0, vocab_pad - vocab), (0, LANES - width - 1)))
+    iw = (
+        input_weight.reshape(width, 4, runs, 2, LANES)
+        .transpose(3, 0, 1, 2, 4)
+        .reshape(2, width, cols)
+    )
+    iw = jnp.pad(iw, ((0, 0), (0, LANES - width), (0, 0)))
+    gate_b = gate_bias.reshape(4, runs, 2, LANES).transpose(2, 0, 1, 3).reshape(2, 1, cols)
+    dec = jnp.pad(decoder_weight.reshape(dec_rows, vocab), ((0, 0), (0, vocab_pad - vocab)))
+    dec_b = jnp.pad(
+        decoder_bias.reshape(1, vocab), ((0, 0), (0, vocab_pad - vocab)), constant_values=-1e30
+    )
+
+    vmem = pl.BlockSpec(memory_space=pltpu.VMEM)
+    dims = (steps, rows, units, vocab_pad, tokens_all, block)
+
+    def sems(*shape):
+        return pltpu.SemaphoreType.DMA((2,) + shape)
+
+    out_rec, out_iw, out_emb, out_dec, out_small = pl.pallas_call(
+        functools.partial(layer_kernel, dims),
+        out_shape=[
+            jax.ShapeDtypeStruct((block, 2 * cols), f32),
+            jax.ShapeDtypeStruct((giw_rows, 2 * cols), f32),
+            jax.ShapeDtypeStruct((8, emb_rows, LANES), f32),
+            jax.ShapeDtypeStruct((dec_rows, vocab_pad), f32),
+            jax.ShapeDtypeStruct((8, vocab_pad), f32),
+        ],
+        in_specs=[vmem] * 7,
+        out_specs=[vmem] * 5,
+        scratch_shapes=[
+            pltpu.VMEM((2, row_count, LANES), jnp.int32),
+            pltpu.VMEM((8, units, cols), bf16),
+            pltpu.VMEM((8, units, vocab_pad), bf16),
+            pltpu.VMEM((8, steps, rows, units), bf16),
+            pltpu.VMEM((steps, rows, cols), f32),
+            pltpu.VMEM((steps, rows, units), f32),
+            pltpu.VMEM((steps, rows, vocab_pad), bf16),
+            pltpu.VMEM((steps, rows, LANES), bf16),
+            pltpu.VMEM((steps, rows, LANES), f32),
+            pltpu.VMEM((steps, rows, LANES), jnp.int32),
+            pltpu.VMEM((steps, rows, vocab_pad), bf16),
+            pltpu.VMEM((steps, rows, cols), bf16),
+            pltpu.VMEM((steps - 1, rows, cols), bf16),
+            pltpu.VMEM((rows, units), f32),
+            pltpu.VMEM((4, part, units), f32),
+            pltpu.VMEM((SPLIT, part, units), f32),
+            pltpu.VMEM((steps - 1, SPLIT, 4, part, units), bf16),
+            pltpu.VMEM((steps - 1, SPLIT, 4, part, units), bf16),
+            pltpu.VMEM((steps - 1, SPLIT, 3, part, units), bf16),
+            pltpu.VMEM((steps - 1, SPLIT, 3, part, units), bf16),
+            pltpu.VMEM((8, vocab_pad), f32),
+            pltpu.VMEM((2, LANES, cols), f32),
+            pltpu.VMEM((4, 2, LANES, cols), f32),
+            pltpu.VMEM((4, 2, LANES, cols), bf16),
+            pltpu.VMEM((4, 2, LANES, cols), bf16),
+            pltpu.VMEM((3, 2, LANES, cols), bf16),
+            pltpu.VMEM((3, 2, LANES, cols), bf16),
+            pltpu.VMEM((giw_rows, cols), f32),
+            pltpu.VMEM((2, giw_rows, units), bf16),
+            pltpu.VMEM((2, giw_rows, units), bf16),
+            pltpu.VMEM((giw_rows, units), bf16),
+            pltpu.VMEM((giw_rows, units), bf16),
+            pltpu.VMEM((2, 4, giw_rows, units), bf16),
+            pltpu.VMEM((8, emb_rows, LANES), f32),
+            pltpu.VMEM((8, emb_rows, LANES), f32),
+            pltpu.VMEM((4, emb_rows, LANES), f32),
+            pltpu.VMEM((8, emb_rows, LANES), f32),
+            pltpu.VMEM((4, dec_rows, vocab_pad), f32),
+            pltpu.VMEM((4, dec_rows, vocab_pad), f32),
+            pltpu.VMEM((4, 8, vocab_pad), f32),
+            sems(1),
+            sems(3, PIECES),
+            sems(4, PIECES),
+            sems(3),
+            sems(7),
+            sems(steps, SPLIT, 4),
+            sems(steps, SPLIT, 3),
+            sems(steps - 1, SPLIT),
+            sems(steps - 1, SPLIT, 3),
+            sems(4, 2),
+            sems(3, 2),
+            sems(5),
+            sems(7),
+            sems(3),
+            sems(7),
+            sems(3),
+            sems(3),
+        ],
+        compiler_params=pltpu.CompilerParams(
+            collective_id=0, has_side_effects=True, vmem_limit_bytes=62 << 20
+        ),
+    )(ids, rec, emb, iw, gate_b, dec, dec_b)
+
+    rec_grad = out_rec.reshape(recurrent_weight.shape)
+    in_grad = out_iw[:width].reshape(input_weight.shape)
+    bias_grad = out_iw[width].reshape(gate_bias.shape)
+    emb_grad = out_emb.reshape(8 * emb_rows, LANES)[:vocab, :width]
+    dec_grad = out_dec[:, :vocab].reshape(decoder_weight.shape)
+    return (
+        out_small[1, 0],
+        emb_grad,
+        in_grad,
+        rec_grad,
+        bias_grad,
+        dec_grad,
+        out_small[0, :vocab],
+    )
 
 
 def on_device(
@@ -15,8 +831,6 @@
     decoder_weight,
     decoder_bias,
 ):
-    f32 = jnp.float32
-    bf16 = jnp.bfloat16
     highest = lax.Precision.HIGHEST
     data_count = lax.axis_size("dp")
     row_count, step_count = char_ids.shape
@@ -86,9 +900,6 @@
         scatter_dimension=0,
         tiled=True,
     ).reshape(decoder_weight.shape)
-    back_matrix = lax.all_gather(recurrent_weight, "dp", axis=0, tiled=True).reshape(
-        hidden_total, gate_cols
-    )
     prev_cells = (
         jnp.concatenate([jnp.zeros((1, row_count, local_units), f32), cells[:-1]], axis=0)
         * keep_mask[:, :, None]
@@ -115,7 +926,7 @@
             .astype(bf16)
         )
         back_term = lax.dot_general(
-            preact_grad, back_matrix, (((1,), (1,)), ((), ())), preferred_element_type=f32
+            preact_grad, rec_matrix, (((1,), (1,)), ((), ())), preferred_element_type=f32
         )
         next_hidden = (
             lax.psum_scatter(back_term, "mp", scatter_dimension=1, tiled=True) * keep_now[:, None]
@@ -181,6 +992,11 @@
         P("mp", "dp", None, None),
         P(),
     )
+    fits = (mesh.shape["dp"], mesh.shape["mp"]) == (8, 4)
     return jax.shard_map(
-        on_device, mesh=mesh, in_specs=in_specs, out_specs=out_specs, check_vma=False
-    )
+        grouped if fits else on_device,
+        mesh=mesh,
+        in_specs=in_specs,
+        out_specs=out_specs,
+        check_vma=False,
+    )

time: 1050 us -> 285 us (0.27)
  waiting for transfers between devices: 702 us -> 0 us
  Pallas kernels: 0 us -> 259 us
  matrix products: 108 us -> 0 us
  blocking collectives: 101 us -> 0 us
  local copies, waits for them, and re-layouts: 67.6 us -> 21.2 us
  other arithmetic: 48.2 us -> 2.27 us
  between operations: 15 us -> 0.72 us
    reduce_scatter x8 -> x0, waiting for transfers between devices: 486 us -> none  [the longest x1 280 us: on_device(): lax.psum_scatter(lax.dot_general(columns, flat_pgrad, (((0,), (0,)), ((),...]
    pallas_call x0 -> x1, Pallas kernels: none -> 259 us  [grouped(): pl.pallas_call(functools.partial(layer_kernel, dims), out_shape=[jax.Shap...]
    psum x3 -> x0, waiting for transfers between devices: 125 us -> none  [the longest x1 62.2 us: on_device(): lax.psum((table_part, dec_bias_part, loss_part), 'dp')]
    dot_general x20 -> x0, matrix products: 108 us -> none  [the longest x6 44.1 us: backward_step(): lax.dot_general(preact_grad, back_matrix, (((1,), (1,)), ((), ())), prefe...]
    all_gather x1 -> x0, waiting for transfers between devices: 90 us -> none  [on_device(): lax.all_gather(recurrent_weight, 'dp', axis=0, tiled=True)]
    all_gather x7 -> x0, blocking collectives: 72.2 us -> none  [the longest x6 44.5 us: forward_step(): hidden_full = lax.all_gather(hidden_loc, 'mp', axis=1, tiled=True)]
    psum x2 -> x0, blocking collectives: 28.9 us -> none  [the longest x1 19.5 us: on_device(): lax.psum((table_part, dec_bias_part, loss_part), 'dp')]
    mul x13 -> x0, other arithmetic: 15.2 us -> none  [the longest x6 7.69 us: backward_step(): next_cell = cell_grad * forget_gate * keep_now[:, None]]
  transfers between devices with their start and end apart: 12 -> 0, of which waited for: 12 -> 0; matrix products, arithmetic and copies ran while one was open for 4% -> 0% of each run, Pallas kernels for 0% -> 0%
where the time goes in v1:
time: 285 us; the launch traced here: 283 us
  Pallas kernels  259 us (91%)
  local copies, waits for them, and re-layouts  21.2 us (7%)
    pallas_call x1, Pallas kernels, grouped(): pl.pallas_call(functools.partial(layer_kernel, dims), out_shape=[jax.Shap...  259 us

profile of v1, /device:TPU:1, one launch (start us, length us, event | category | flops | bytes accessed | tf_op | source)
XLA Modules:
  0.0 283.0 jit_solution(13349255933570754348)
XLA Ops:
  0.6 0.0 copy-start.1
  0.6 0.8 reshape.57
  1.4 0.6 pad.25.decb_ref
  2.0 0.7 reshape.54
  2.7 0.6 copy.31
  3.3 0.7 pad_add_fusion
  4.0 1.4 pad.24.dec_ref
  5.5 0.1 copy.28
  5.6 0.6 pad.21.ids_ref
  6.2 1.5 fusion.2.emb_ref
  7.7 1.2 reshape.52
  8.9 0.2 copy.35
  9.1 0.2 reshape.53
  9.4 0.9 pad.23.iw_ref
  10.2 0.0 copy-done.1
  10.2 0.4 reshape.50
  10.7 0.5 copy.34
  11.2 1.5 reshape.51.rec_ref
  12.8 258.8 %shard_map.144 = (f32[256,2048]{1,0:T(8,128)}, f32[112,2048]{1,0:T(8,128)}, f32[8,40,128]{2,1,0:T(8,128)}, f32[64,384]{1,0:T(8,128)}, f32[8,384]{1,0:T(8,128)}) custom-call(s32[128,128]{1,0:T(8,128)} %pad.21.ids_ref, bf16[2,256,1024]{2,1,0:T(8,128)(2,1)} %reshape.51.rec_ref, bf16[384,128]{1,0:T(8,128)(2,1)} %fusion.2.emb_ref, ...), custom_call_target="tpu_custom_call" | custom-call | tf_op jit(solution)/shard_map/pallas_call | solution.py:732
  271.5 0.0 copy-start.2
  271.5 0.0 copy-start
  271.6 1.3 slice.18
  272.9 1.6 slice.24
  274.5 1.3 slice_reduce_fusion.1
  275.8 0.9 slice_reduce_fusion
  276.6 1.2 slice.20
  277.9 1.4 reshape.59
  279.3 0.6 reshape_squeeze.3
  279.9 0.0 copy-done.2
  279.9 0.6 slice_bitcast_fusion
  280.6 0.0 copy-done
  280.6 2.4 reshape.60
Async XLA Ops:
  0.6 9.6 %copy-start.1 = (bf16[256,4,512]{2,1,0:T(4,128)(2,1)S(1)}, bf16[256,4,512]{2,1,0:T(4,128)(2,1)}, u32[]{:S(2)}) copy-start(bf16[256,4,512]{2,1,0:T(4,128)(2,1)} %param.14) | copy-start | bytes 3145732
  271.5 8.4 %copy-start.2 = (f32[64,384]{1,0:T(8,128)S(1)}, f32[64,384]{1,0:T(8,128)}, u32[]{:S(2)}) copy-start(f32[64,384]{1,0:T(8,128)} %get-tuple-element.16) | copy-start | bytes 294916
  271.5 9.0 %copy-start = (f32[256,2048]{1,0:T(8,128)S(1)}, f32[256,2048]{1,0:T(8,128)}, u32[]{:S(2)}) copy-start(f32[256,2048]{1,0:T(8,128)} %get-tuple-element.15) | copy-start | bytes 6291460

commit v2 on v1

v2 whole, which is shorter than its diff:
```python
import functools

import jax
import jax.numpy as jnp
from jax import lax
from jax.experimental import pallas as pl
from jax.experimental.pallas import tpu as pltpu
from jax.sharding import PartitionSpec as P

f32 = jnp.float32
bf16 = jnp.bfloat16
MESH = pl.DeviceIdType.MESH
LANES = 128
CHIPS = ((2, 0), (0, 2), (2, 2))
PEERS = ((0, 1), (2, 0), (0, 2), (2, 2), (2, 1), (0, 3), (2, 3), (1, 0), (4, 0), (5, 0), (6, 0))
GROUP = ((0, 1), (2, 0), (0, 2), (2, 2), (2, 1), (0, 3), (2, 3))
OTHERS = (1, 4, 5)
COLUMN = (4, 6, 2)
SPLIT = 2
PIECES = 8
SUB = 2


def turn(value, flips):
    for bit in (1, 2, 4):
        if flips & bit:
            value = value + bit - 2 * bit * lax.rem(lax.div(value, bit), 2)
    return value


def dot(a, b):
    return jnp.dot(a, b, preferred_element_type=f32)


def dot_t(a, b):
    return lax.dot_general(a, b, (((1,), (1,)), ((), ())), preferred_element_type=f32)


def t_dot(a, b):
    return lax.dot_general(a, b, (((0,), (0,)), ((), ())), preferred_element_type=f32)


def layer_kernel(
    dims,
    chars_ref,
    nexts_ref,
    resets_ref,
    emb_ref,
    iw_ref,
    rec_ref,
    gb_ref,
    dec_ref,
    decb_ref,
    out_loss,
    out_emb,
    out_iw,
    out_rec,
    out_gb,
    out_dec,
    out_decb,
    ids_rows,
    ids_cols,
    rec_halves,
    weights,
    emb_pad,
    iw_pads,
    gb_pads,
    dec_pad,
    decb_pad,
    dec_all,
    hid,
    gates,
    cells,
    onehots,
    embedded,
    keeps,
    targets,
    logit_grads,
    pgs,
    pgm,
    carry_c,
    pg_now,
    pg_out,
    pgm_out,
    pgm_now,
    own_sum,
    chip_out,
    chip_in,
    small_acc,
    small_pair,
    both,
    acc,
    x_out,
    x_in,
    z_out,
    z_in,
    giw_acc,
    giw_out,
    giw_x_in,
    giw_z_out,
    giw_z_in,
    giw_full,
    emb_part,
    emb_in,
    emb_sums,
    emb_full,
    dec_part,
    dec_x_out,
    dec_x_in,
    dec_z_out,
    dec_z_in,
    ids_sem,
    wz_sem,
    wx_sem,
    wc_sem,
    iw_sem,
    decg_sem,
    decr_sem,
    hid_sem,
    hidc_sem,
    lg_sem,
    pg_sem,
    pgm_sem,
    small_sem,
    chip_sem,
    gx_sem,
    gz_sem,
    giw_sem,
    emb_sem,
    emb2_sem,
    emb3_sem,
    dsum_sem,
):
    steps, rows, units, vocab, vocab_pad, tokens_all, block = dims
    cols = 4 * units
    half = rows // 2
    part = half // SPLIT
    d, m = lax.axis_index("dp"), lax.axis_index("mp")
    x_at, z_low, z_high = lax.rem(d, 2), lax.rem(lax.div(d, 2), 2), lax.div(d, 4)
    z_at = lax.div(d, 2)
    core, y_at = lax.rem(m, 2), lax.div(m, 2)

    def device(flips):
        return (turn(d, flips[0]), turn(m, flips[1]))

    def slot(flips):
        return turn(z_low, flips[0] // 2) * 4 + turn(m, flips[1])

    def chip(flips):
        return pl.ds(turn(z_low, flips[0] // 2) * 4 + turn(y_at, flips[1] // 2) * 2, 2)

    own = slot((0, 0))

    def copy(src, dst, sems, at, flips):
        return pltpu.make_async_remote_copy(
            src_ref=src,
            dst_ref=dst,
            send_sem=sems.at[(0,) + at],
            recv_sem=sems.at[(1,) + at],
            device_id=device(flips),
            device_id_type=MESH,
        )

    barrier = pltpu.get_barrier_semaphore()
    for flips in PEERS:
        pl.semaphore_signal(barrier, inc=1, device_id=device(flips), device_id_type=MESH)
    pl.semaphore_wait(barrier, len(PEERS))

    piece = block // PIECES

    def weight_rows(index, p):
        first = p * piece
        side, inside = first // LANES, first % LANES
        return weights.at[
            core,
            side * 4 + lax.div(index, 2),
            pl.ds(pl.multiple_of(lax.rem(index, 2) * LANES + inside, piece), piece),
        ]

    def weight_core(index, at, p):
        spot = weight_rows(index, p)
        return copy(spot, spot, wc_sem, (at, p), (0, 1))

    def block_of(at):
        return turn(d, (0, 4, 6, 2)[at % 4] + at // 4)

    def weight_z(k, p):
        flips = COLUMN[k]
        half = turn(z_low, (flips & 2) // 2)
        return copy(
            rec_halves.at[half, pl.ds(p * piece, piece)], weight_rows(d, p), wz_sem, (k, p), (flips, 0)
        )

    def weight_z_in(k, p):
        spot = weight_rows(turn(d, COLUMN[k]), p)
        return copy(spot, spot, wz_sem, (k, p), (COLUMN[k], 0))

    def weight_x(k, p):
        if k == 3:
            return copy(
                rec_halves.at[z_low, pl.ds(p * piece, piece)],
                weight_rows(d, p),
                wx_sem,
                (k, p),
                (1, 0),
            )
        spot = weight_rows(turn(d, COLUMN[k]), p)
        return copy(spot, spot, wx_sem, (k, p), (1, 0))

    def weight_x_in(k, p):
        flips = 0 if k == 3 else COLUMN[k]
        spot = weight_rows(turn(d, flips + 1), p)
        return copy(spot, spot, wx_sem, (k, p), (1, 0))

    runs = units // LANES
    width = iw_ref.shape[1]
    dec_rows = dec_ref.shape[0]
    vocab_rows = emb_pad.shape[0]

    def dec_spot(flips):
        at = turn(z_high, flips // 4) * LANES + turn(x_at, flips % 2) * dec_rows
        return dec_all.at[own, pl.ds(pl.multiple_of(at, dec_rows), dec_rows)]

    ids_rows[z_low, 0:steps] = chars_ref[...]
    ids_rows[z_low, 8 : 8 + steps] = nexts_ref[...]
    ids_rows[z_low, 16 : 16 + steps] = resets_ref[...]
    ids_copy = copy(ids_rows.at[z_low], ids_rows.at[z_low], ids_sem, (0,), (2, 0))
    ids_copy.start()
    for p in range(PIECES):
        here = slice(p * piece, (p + 1) * piece)
        for gate in range(4):
            for run in range(runs):
                for side in range(2):
                    at = (run * 2 + side) * LANES
                    to = gate * units + run * LANES
                    rec_halves[side, here, to : to + LANES] = rec_ref[gate, here, at : at + LANES]
        for k in range(3):
            weight_z(k, p).start()
        weight_x(3, p).start()
        if p == 0:
            dec_pad[...] = jnp.zeros_like(dec_pad)
            dec_pad[:, :vocab] = dec_ref[...]
            dec_z = copy(dec_pad, dec_spot(0), decg_sem, (0,), (4, 0))
            dec_z.start()
            dec_x = [copy(dec_pad, dec_spot(0), decg_sem, (1,), (1, 0))]
            dec_x[0].start()

    def weight_round(p):
        for k in range(3):
            weight_z_in(k, p).wait_recv()
            weight_x(k, p).start()
            weight_core(block_of(1 + k), 1 + k, p).start()
        if p:
            weight_over_x(p - 1)

    def weight_over_x(p):
        for k in (3, 0, 1, 2):
            weight_x_in(k, p).wait_recv()
            at = 4 if k == 3 else 5 + k
            weight_core(block_of(at), at, p).start()

    for p in range(PIECES):
        weight_rows(d, p)[...] = rec_halves[z_low, pl.ds(p * piece, piece)]
        weight_core(block_of(0), 0, p).start()
    dec_spot(0)[...] = dec_pad[...]
    emb_pad[...] = jnp.zeros_like(emb_pad)
    emb_pad[:vocab, :width] = emb_ref[...]
    ones_at = lax.broadcasted_iota(jnp.int32, emb_pad.shape, 1) == width
    emb_pad[...] = jnp.where(ones_at, 1.0, emb_pad[...].astype(f32)).astype(bf16)
    iw_pads[core] = jnp.zeros(iw_pads.shape[1:], bf16)

    def half_lanes(run):
        return pl.ds(pl.multiple_of((run * 2 + z_low) * LANES, LANES), LANES)

    for gate in range(4):
        for run in range(runs):
            to = gate * units + run * LANES
            iw_pads[core, :width, to : to + LANES] = iw_ref[gate, :, half_lanes(run)]
            gb_pads[core, :, to : to + LANES] = gb_ref[gate : gate + 1, half_lanes(run)]
    iw_copies = [
        copy(ref.at[core], ref.at[core], iw_sem, (k,), (0, 1))
        for k, ref in enumerate((iw_pads, gb_pads))
    ]
    for each in iw_copies:
        each.start()
    decb_pad[...] = jnp.full(decb_pad.shape, -1e30, f32)
    decb_pad[:, :vocab] = decb_ref[...]
    ids_copy.wait_recv()
    ids_cols[...] = ids_rows[core].T
    vocab_iota = lax.broadcasted_iota(jnp.int32, (vocab_rows, rows), 0)

    def read_ids(t):
        now = jnp.concatenate([ids_rows[0, t : t + 1], ids_rows[1, t : t + 1]], axis=1)
        onehots[t] = (vocab_iota == now).astype(f32).astype(bf16)
        targets[t] = jnp.broadcast_to(ids_cols[:, 8 + t : 9 + t], (half, LANES))
        keeps[t] = jnp.broadcast_to((1 - ids_cols[:, 16 + t : 17 + t]).astype(f32), (half, LANES))

    def project(t):
        read_ids(t)
        chosen = t_dot(onehots[t], emb_pad[...]).astype(bf16)
        embedded[t] = chosen
        mine = embedded[t, pl.ds(pl.multiple_of(core * half, half), half)]
        for c in range(2):
            gates[t, c] = dot(mine, iw_pads[c]) + gb_pads[c]

    for k, ref in enumerate((iw_pads, gb_pads)):
        copy(ref.at[1 - core], ref.at[1 - core], iw_sem, (k,), (0, 1)).wait_recv()
    project(0)

    def span(s):
        return pl.ds(s * part, part)

    def wide(s):
        return pl.ds(pl.multiple_of(core * half + s * part, part), part)

    def hidden_copy(t, s, j):
        spot = hid.at[chip((0, 0)), t, wide(s)]
        return copy(spot, spot, hid_sem, (t, s, j), CHIPS[j])

    def hidden_in(t, s, j):
        spot = hid.at[chip(CHIPS[j]), t, wide(s)]
        return copy(spot, spot, hid_sem, (t, s, j), CHIPS[j])

    def hidden_core(t, s):
        spot = hid.at[:, t, wide(s)]
        return copy(spot, spot, hidc_sem, (t, s), (0, 1))

    def hidden_core_in(t, s):
        rows_there = pl.ds(pl.multiple_of((1 - core) * half + s * part, part), part)
        spot = hid.at[:, t, rows_there]
        return copy(spot, spot, hidc_sem, (t, s), (0, 1))

    def cell_step(t, s, added):
        here = span(s)
        if added is not None:
            keep = keeps[t, here, :1]
        for c in range(2):
            preact = gates[t, c, here]
            if added is not None:
                preact = preact + keep * added[c]
            in_gate = jax.nn.sigmoid(preact[:, :units])
            forget = jax.nn.sigmoid(preact[:, units : 2 * units])
            candidate = jnp.tanh(preact[:, 2 * units : 3 * units])
            out_gate = jax.nn.sigmoid(preact[:, 3 * units :])
            cell = in_gate * candidate
            if added is not None:
                cell = forget * keep * cells[t - 1, c, here] + cell
            cells[t, c, here] = cell
            hid[z_low * 4 + y_at * 2 + c, t, wide(s)] = (out_gate * jnp.tanh(cell)).astype(bf16)
            gates[t, c, here, :units] = in_gate
            gates[t, c, here, units : 2 * units] = forget
            gates[t, c, here, 2 * units : 3 * units] = candidate
            gates[t, c, here, 3 * units :] = out_gate
        for j in (2, 0, 1):
            hidden_copy(t, s, j).start()

    for s in range(SPLIT):
        cell_step(0, s, None)

    weight_round(0)
    project(1)
    project(2)
    weight_round(1)
    spot = dec_spot(4)
    copy(spot, spot, decg_sem, (0,), (4, 0)).wait_recv()
    dec_x.append(copy(spot, spot, decg_sem, (2,), (1, 0)))
    dec_x[1].start()
    project(3)
    weight_round(2)
    project(4)
    project(5)
    weight_round(3)
    for j, flips in enumerate((1, 5)):
        spot = dec_spot(flips)
        copy(spot, spot, decg_sem, (1 + j,), (1, 0)).wait_recv()
    dec_own = dec_all.at[own]
    dec_sends = [
        copy(dec_own, dec_own, decr_sem, (j,), flips) for j, flips in enumerate(CHIPS + ((0, 1),))
    ]
    for each in dec_sends:
        each.start()
    weight_round(4)
    weight_round(5)
    dec_relays = []
    for j in range(3):
        spot = dec_all.at[slot(CHIPS[j])]
        copy(spot, spot, decr_sem, (j,), CHIPS[j]).wait_recv()
        each = copy(spot, spot, decr_sem, (4 + j,), (0, 1))
        each.start()
        dec_relays.append(each)
    for p in range(6, PIECES):
        weight_round(p)
    spot = dec_all.at[slot((0, 1))]
    copy(spot, spot, decr_sem, (3,), (0, 1)).wait_recv()
    for j in range(3):
        spot = dec_all.at[slot((CHIPS[j][0], CHIPS[j][1] + 1))]
        copy(spot, spot, decr_sem, (4 + j,), (0, 1)).wait_recv()
    weight_over_x(PIECES - 1)
    for p in range(PIECES):
        for at in range(8):
            spot = weights.at[
                1 - core,
                (p * piece // LANES) * 4 + lax.div(block_of(at), 2),
                pl.ds(
                    pl.multiple_of(
                        lax.rem(block_of(at), 2) * LANES + p * piece % LANES, piece
                    ),
                    piece,
                ),
            ]
            copy(spot, spot, wc_sem, (at, p), (0, 1)).wait_recv()

    def add_chip(total, t, s, flips):
        first = turn(z_low, flips[0] // 2) * 4 + turn(y_at, flips[1] // 2) * 2
        for k in range(2):
            some = hid[first + k, t, wide(s)]
            for c in range(2):
                more = dot(some, weights[c, first + k])
                total[c] = more if total[c] is None else total[c] + more

    def gather_hidden(t, s):
        total = [None, None]
        add_chip(total, t, s, (0, 0))
        for j in range(3):
            hidden_in(t, s, j).wait_recv()
            add_chip(total, t, s, CHIPS[j])
        hidden_core(t, s).start()
        return total

    vocab_part = lax.broadcasted_iota(jnp.int32, (part, vocab_pad), 1)
    last_lane = lax.broadcasted_iota(jnp.int32, (1, vocab_pad), 1) == vocab_pad - 1
    small_acc[...] = jnp.zeros_like(small_acc)

    def lg_copy(t, s):
        spot = logit_grads.at[t, wide(s)]
        return copy(spot, spot, lg_sem, (t, s), (0, 1))

    def decode(t, s):
        here = span(s)
        logits = decb_pad[...]
        for at in range(8):
            logits = logits + dot(hid[at, t, wide(s)], dec_all[at])
        top = jnp.max(logits, axis=1, keepdims=True)
        exps = jnp.exp(logits - top)
        total = jnp.sum(exps, axis=1, keepdims=True)
        hot = targets[t, here, :1] == vocab_part
        picked = jnp.sum(jnp.where(hot, logits, 0.0), axis=1, keepdims=True)
        lost = top + jnp.log(total) - picked
        grad = ((exps / total - jnp.where(hot, 1.0, 0.0)) / tokens_all).astype(bf16)
        logit_grads[t, wide(s)] = grad
        lg_copy(t, s).start()
        small_acc[...] += jnp.sum(grad.astype(f32), axis=0, keepdims=True) + jnp.where(
            last_lane, jnp.sum(lost, axis=0, keepdims=True) / tokens_all, 0.0
        )

    def forward(t, _):
        for s in range(SPLIT):
            cell_step(t, s, gather_hidden(t - 1, s))
            decode(t - 1, s)
        return 0

    lax.fori_loop(1, steps, forward, 0)

    def pg_copy(t, s):
        return copy(pg_out.at[t, span(s)], pgs.at[t, wide(s)], pg_sem, (t, s), (0, 1))

    def pgm_copy(t, s):
        return copy(
            pgm_out.at[t - 1, span(s)], pgm.at[t - 1, wide(s)], pgm_sem, (t - 1, s), (0, 1)
        )

    def cell_back(t, s, carried, first):
        here = span(s)
        if not first:
            keep = keeps[t, here, :1]
        for c in range(2):
            hidden_grad = dot_t(logit_grads[t, wide(s)], dec_all[z_low * 4 + y_at * 2 + c])
            if carried is not None:
                hidden_grad = hidden_grad + carried[:, c * units : (c + 1) * units]
            in_gate = gates[t, c, here, :units]
            forget = gates[t, c, here, units : 2 * units]
            candidate = gates[t, c, here, 2 * units : 3 * units]
            out_gate = gates[t, c, here, 3 * units :]
            squash = jnp.tanh(cells[t, c, here])
            cell_grad = hidden_grad * out_gate * (1.0 - squash * squash)
            if carried is not None:
                cell_grad = cell_grad + carry_c[c, here]
            grads = [
                cell_grad * candidate * in_gate * (1.0 - in_gate),
                None,
                cell_grad * in_gate * (1.0 - candidate * candidate),
                hidden_grad * squash * out_gate * (1.0 - out_gate),
            ]
            if first:
                grads[1] = jnp.zeros_like(cell_grad)
            else:
                grads[1] = cell_grad * (keep * cells[t - 1, c, here]) * forget * (1.0 - forget)
                carry_c[c, here] = keep * forget * cell_grad
            for k in range(4):
                pg_now[c, here, k * units : (k + 1) * units] = grads[k].astype(bf16)
                if not first:
                    pgm_now[c, here, k * units : (k + 1) * units] = (keep * grads[k]).astype(bf16)

    def share(t, s, first):
        here = span(s)
        pgs[t, wide(s)] = pg_now[core, here]
        pg_out[t, here] = pg_now[1 - core, here]
        if not first:
            pgm[t - 1, wide(s)] = pgm_now[core, here]
            pgm_out[t - 1, here] = pgm_now[1 - core, here]
            pgm_copy(t, s).start()
        pg_copy(t, s).start()

    def chip_copy(t, s, j):
        return copy(
            chip_out.at[t - 1, s, j], chip_in.at[t - 1, s, j], chip_sem, (t - 1, s, j), CHIPS[j]
        )

    def spread(t, s):
        here = span(s)
        for j in (2, 0, 1, 3):
            flips = CHIPS[j] if j < 3 else (0, 0)
            first = turn(z_low, flips[0] // 2) * 4 + turn(y_at, flips[1] // 2) * 2
            for k in range(2):
                part_sum = dot_t(pgm_now[0, here], weights[0, first + k]) + dot_t(
                    pgm_now[1, here], weights[1, first + k]
                )
                lanes = slice(k * units, (k + 1) * units)
                if j < 3:
                    chip_out[t - 1, s, j, :, lanes] = part_sum.astype(bf16)
                else:
                    own_sum[s, :, lanes] = part_sum
            if j < 3:
                chip_copy(t, s, j).start()

    def carried_in(t, s):
        total = own_sum[s]
        for j in range(3):
            chip_copy(t + 1, s, j).wait_recv()
            total = total + chip_in[t, s, j].astype(f32)
        return total

    last = steps - 1
    for s in range(SPLIT):
        for j in range(3):
            hidden_in(last, s, j).wait_recv()
        hidden_core(last, s).start()
        decode(last, s)
        cell_back(last, s, None, False)
        spread(last, s)
        share(last, s, False)

    def backward(i, _):
        t = last - i
        for s in range(SPLIT):
            cell_back(t, s, carried_in(t, s), False)
            spread(t, s)
            share(t, s, False)
        return 0

    lax.fori_loop(1, last, backward, 0)

    far = (2, 3, 1, 0)

    piece_rows = LANES // SUB

    def x_copy(k, side, sub):
        here = pl.ds(sub * piece_rows, piece_rows)
        return copy(
            x_out.at[k, side, here], x_in.at[k, side, here], gx_sem, (k, side, sub), (1, 0)
        )

    def z_copy(k, side, sub):
        here = pl.ds(sub * piece_rows, piece_rows)
        return copy(
            z_out.at[k, side, here], z_in.at[k, side, here], gz_sem, (k, side, sub), (far[k] * 2, 0)
        )

    used = (steps - 1) * rows

    def from_core(t, first):
        for s in range(SPLIT):
            hidden_core_in(t, s).wait_recv()
            rows_there = pl.ds(pl.multiple_of((1 - core) * half + s * part, part), part)
            spot = logit_grads.at[t, rows_there]
            copy(spot, spot, lg_sem, (t, s), (0, 1)).wait_recv()
            spot = pgs.at[t, rows_there]
            copy(spot, spot, pg_sem, (t, s), (0, 1)).wait_recv()
            if not first:
                spot = pgm.at[t - 1, rows_there]
                copy(spot, spot, pgm_sem, (t - 1, s), (0, 1)).wait_recv()

    def all_from_core(t, _):
        from_core(t, False)
        return 0

    lax.fori_loop(1, steps, all_from_core, 0)
    hidden_0 = [hidden_core_in(0, s) for s in range(SPLIT)]
    for each in hidden_0:
        each.wait_recv()

    def weight_grad(k, side):
        at = side * 4 + turn(z_at, far[k])
        both[...] = t_dot(
            hid[at, 0 : steps - 1].reshape(used, units), pgm[...].reshape(used, cols)
        ).reshape(2, LANES, cols)
        x_out[k, side] = both[1 - x_at].astype(bf16)
        acc[k, side] = both[x_at]

    order = [(k, side, sub) for k in range(4) for side in range(2) for sub in range(SUB)]

    def send_x(first, last):
        for spot in order[first:last]:
            x_copy(*spot).start()

    def pass_z(at):
        k, side, sub = order[at]
        here = pl.ds(sub * piece_rows, piece_rows)
        x_copy(k, side, sub).wait_recv()
        total = acc[k, side, here] + x_in[k, side, here].astype(f32)
        if k == 3:
            acc[k, side, here] = total
            return
        z_out[k, side, here] = total.astype(bf16)
        if at in range(2, 4 * SUB):
            z_copy(*order[at - 2]).wait_send()
        z_copy(k, side, sub).start()

    weight_grad(0, 0)
    send_x(0, SUB)
    weight_grad(0, 1)
    send_x(SUB, 2 * SUB)
    weight_grad(1, 0)
    weight_grad(1, 1)
    pass_z(0)

    for s in range(SPLIT):
        cell_back(0, s, carried_in(0, s), True)
        share(0, s, True)
    small_pair[core] = small_acc[...]
    small_copy = copy(small_pair.at[core], small_pair.at[core], small_sem, (0,), (0, 1))
    small_copy.start()
    for s in range(SPLIT):
        rows_there = pl.ds(pl.multiple_of((1 - core) * half + s * part, part), part)
        spot = logit_grads.at[0, rows_there]
        copy(spot, spot, lg_sem, (0, s), (0, 1)).wait_recv()
        spot = pgs.at[0, rows_there]
        copy(spot, spot, pg_sem, (0, s), (0, 1)).wait_recv()
    spot = small_pair.at[1 - core]
    copy(spot, spot, small_sem, (0,), (0, 1)).wait_recv()
    tokens = steps * rows
    giw_rows = giw_acc.shape[0]
    giw_acc[...] = t_dot(
        embedded[...].reshape(tokens, LANES), pgs[...].reshape(tokens, cols)
    )[:giw_rows]
    for k in range(2):
        at = pl.multiple_of((1 - x_at) * (2 * units) + k * units, units)
        giw_out[k] = giw_acc[:, pl.ds(at, units)].astype(bf16)
    giw_x = copy(giw_out, giw_x_in, giw_sem, (0,), (1, 0))
    giw_x.start()
    dec_part[...] = t_dot(
        hid[own].reshape(tokens, units), logit_grads[...].reshape(tokens, vocab_pad)
    ).reshape(2, 2, dec_rows, vocab_pad)
    for k in range(2):
        dec_x_out[k] = dec_part[k, 1 - x_at].astype(bf16)
    dsum_x = copy(dec_x_out, dec_x_in, dsum_sem, (0,), (1, 0))
    dsum_x.start()
    send_x(2 * SUB, 3 * SUB)
    pass_z(1)

    emb_rows = emb_full.shape[1]
    by_char = jnp.zeros((vocab_rows, 2 * LANES), f32)
    for t in range(steps):
        by_token = dot_t(pgs[t], iw_pads[core])
        high = by_token.astype(bf16)
        low = (by_token - high.astype(f32)).astype(bf16)
        by_char = by_char + dot(onehots[t], jnp.concatenate([high, low], axis=1))
    emb_part[...] = (by_char[:, :LANES] + by_char[:, LANES:]).reshape(8, emb_rows, LANES)
    emb_copies = [
        copy(emb_part.at[slot(flips)], emb_in.at[own], emb_sem, (j,), flips)
        for j, flips in enumerate(GROUP)
    ]
    for each in emb_copies:
        each.start()
    emb_in[own] = emb_part[own]
    pass_z(2)
    send_x(3 * SUB, 4 * SUB)

    giw_x.wait_recv()
    for k in range(2):
        at = pl.multiple_of(x_at * (2 * units) + k * units, units)
        giw_acc[:, pl.ds(at, units)] += giw_x_in[k].astype(f32)
    giw_z_out[...] = giw_acc[
        :, pl.ds(pl.multiple_of(x_at * (2 * units) + (1 - z_high) * units, units), units)
    ].astype(bf16)
    giw_z = copy(giw_z_out, giw_z_in, giw_sem, (1,), (4, 0))
    giw_z.start()
    dsum_x.wait_recv()
    dec_z_out[...] = (
        dec_part[1 - z_high, x_at] + dec_x_in[1 - z_high].astype(f32)
    ).astype(bf16)
    dsum_z = copy(dec_z_out, dec_z_in, dsum_sem, (1,), (4, 0))
    dsum_z.start()
    for j, flips in enumerate(GROUP):
        spot = emb_in.at[slot(flips)]
        copy(spot, spot, emb_sem, (j,), flips).wait_recv()
    total = emb_in[0]
    for at in range(1, 8):
        total = total + emb_in[at]

    def place(flips):
        return turn(z_high, flips // 4) * 2 + turn(x_at, flips % 2)

    emb_sums[place(0), :emb_rows] = total
    smalls = small_pair[0] + small_pair[1]
    for k in range(vocab_pad // LANES):
        emb_sums[place(0), emb_rows + k : emb_rows + k + 1] = smalls[
            :, k * LANES : (k + 1) * LANES
        ]
    spot = emb_sums.at[place(0)]
    emb2 = [copy(spot, spot, emb2_sem, (j,), (flips, 0)) for j, flips in enumerate(OTHERS)]
    for each in emb2:
        each.start()
    pass_z(3)
    weight_grad(2, 0)
    weight_grad(2, 1)
    send_x(4 * SUB, 5 * SUB)
    weight_grad(3, 0)
    weight_grad(3, 1)

    giw_z.wait_recv()
    gate_at = x_at * 2 + z_high
    giw_full[z_low, gate_at] = (
        giw_acc[:, pl.ds(pl.multiple_of(gate_at * units, units), units)] + giw_z_in[...].astype(f32)
    ).astype(bf16)
    spot = giw_full.at[z_low, gate_at]
    giw_back_z = copy(spot, spot, giw_sem, (2,), (4, 0))
    giw_back_z.start()
    pass_z(4)
    send_x(5 * SUB, 6 * SUB)
    for j, flips in enumerate(OTHERS):
        spot = emb_sums.at[place(flips)]
        copy(spot, spot, emb2_sem, (j,), (flips, 0)).wait_recv()
    sums = (emb_sums[0] + emb_sums[1]) + (emb_sums[2] + emb_sums[3])
    emb_full[own] = sums[:emb_rows]
    spot = emb_full.at[own]
    emb3 = [copy(spot, spot, emb3_sem, (j,), flips) for j, flips in enumerate(GROUP)]
    for each in emb3:
        each.start()
    for k in range(vocab_pad // LANES):
        lanes = slice(k * LANES, min(vocab, (k + 1) * LANES))
        out_decb[:, lanes] = sums[emb_rows + k : emb_rows + k + 1, : lanes.stop - lanes.start]
    k = vocab_pad // LANES - 1
    out_loss[...] = sums[emb_rows + k : emb_rows + k + 1, LANES - 1 :]
    pass_z(5)
    spot = giw_full.at[z_low, x_at * 2 + 1 - z_high]
    copy(spot, spot, giw_sem, (2,), (4, 0)).wait_recv()
    spot = giw_full.at[z_low, pl.ds(x_at * 2, 2)]
    giw_back_x = copy(spot, spot, giw_sem, (3,), (1, 0))
    giw_back_x.start()
    send_x(6 * SUB, 8 * SUB)
    pass_z(6)
    dsum_z.wait_recv()
    total = dec_part[z_high, x_at] + dec_x_in[z_high].astype(f32) + dec_z_in[...].astype(f32)
    out_dec[...] = total[:, :vocab]
    spot = giw_full.at[z_low, pl.ds((1 - x_at) * 2, 2)]
    copy(spot, spot, giw_sem, (3,), (1, 0)).wait_recv()
    spot = giw_full.at[z_low]
    giw_side = copy(spot, spot, giw_sem, (4,), (2, 0))
    giw_side.start()
    pass_z(7)
    for j, flips in enumerate(GROUP):
        spot = emb_full.at[slot(flips)]
        copy(spot, spot, emb3_sem, (j,), flips).wait_recv()
    out_emb[...] = emb_full[...].reshape(vocab_rows, LANES)[:vocab, :width]
    for at in range(4 * SUB, 6 * SUB):
        pass_z(at)
    spot = giw_full.at[1 - z_low]
    copy(spot, spot, giw_sem, (4,), (2, 0)).wait_recv()
    for side in range(2):
        for gate in range(4):
            value = giw_full[side, gate].astype(f32)
            for run in range(runs):
                to = slice((run * 2 + side) * LANES, (run * 2 + side + 1) * LANES)
                lanes = slice(run * LANES, (run + 1) * LANES)
                out_iw[gate, :, to] = value[:width, lanes]
                out_gb[gate : gate + 1, to] = value[width : width + 1, lanes]
    for at in range(6 * SUB, 8 * SUB):
        pass_z(at)

    def scatter(here, side, gate, value):
        for run in range(runs):
            at = pl.multiple_of(gate * 2 * units + run * 2 * LANES + side * LANES, LANES)
            out_rec[here, pl.ds(at, LANES)] = value[:, run * LANES : (run + 1) * LANES]

    for side in range(2):
        for sub in range(SUB):
            z_copy(0, side, sub).wait_recv()
            z_copy(1, side, sub).wait_recv()
            z_copy(2, side, sub).wait_recv()
            here = pl.ds(side * LANES + sub * piece_rows, piece_rows)
            mine = pl.ds(sub * piece_rows, piece_rows)
            for gate in range(4):
                lanes = slice(gate * units, (gate + 1) * units)
                scatter(
                    here,
                    z_low,
                    gate,
                    acc[3, side, mine, lanes] + z_in[0, side, mine, lanes].astype(f32),
                )
                scatter(
                    here,
                    1 - z_low,
                    gate,
                    z_in[1, side, mine, lanes].astype(f32) + z_in[2, side, mine, lanes].astype(f32),
                )

    ids_copy.wait_send()
    dec_z.wait_send()
    for each in dec_x + dec_sends + dec_relays + iw_copies + [small_copy]:
        each.wait_send()
    for p in range(PIECES):
        for at in range(8):
            weight_core(block_of(at), at, p).wait_send()
        for k in range(3):
            weight_z(k, p).wait_send()
        for k in range(4):
            weight_x(k, p).wait_send()

    def sent(t, _):
        for s in range(SPLIT):
            for j in range(3):
                hidden_copy(t, s, j).wait_send()
            hidden_core(t, s).wait_send()
            lg_copy(t, s).wait_send()
            pg_copy(t, s).wait_send()
        return 0

    lax.fori_loop(0, steps, sent, 0)

    def sent_back(t, _):
        for s in range(SPLIT):
            pgm_copy(t, s).wait_send()
            for j in range(3):
                chip_copy(t, s, j).wait_send()
        return 0

    lax.fori_loop(1, steps, sent_back, 0)
    for at, spot in enumerate(order):
        x_copy(*spot).wait_send()
        if spot[0] < 3 and at not in range(4 * SUB - 2):
            z_copy(*spot).wait_send()
    for each in [giw_x, giw_z, giw_back_z, giw_back_x, giw_side, dsum_x, dsum_z]:
        each.wait_send()
    for each in emb_copies + emb2 + emb3:
        each.wait_send()


def grouped(
    char_ids,
    next_chars,
    resets,
    embedding,
    input_weight,
    recurrent_weight,
    gate_bias,
    decoder_weight,
    decoder_bias,
):
    data_count = lax.axis_size("dp")
    row_count, steps = char_ids.shape
    vocab, width = embedding.shape
    local_units = input_weight.shape[2]
    block = recurrent_weight.shape[0]
    units = local_units // 2
    cols = 4 * units
    rows = 2 * row_count
    dec_rows = decoder_weight.shape[2]
    vocab_pad = pl.cdiv(vocab, LANES) * LANES
    tokens_all = row_count * steps * data_count
    half = rows // 2
    part = half // SPLIT
    emb_rows = pl.cdiv(vocab, 64) * 8
    giw_rows = pl.cdiv(width + 1, 16) * 16

    vocab_rows = 8 * emb_rows
    by_gate = recurrent_weight.transpose(1, 0, 2)
    in_by_gate = input_weight.transpose(1, 0, 2)
    dec = decoder_weight.reshape(dec_rows, vocab)

    vmem = pl.BlockSpec(memory_space=pltpu.VMEM)
    dims = (steps, rows, units, vocab, vocab_pad, tokens_all, block)

    def sems(*shape):
        return pltpu.SemaphoreType.DMA((2,) + shape)

    loss, emb_grad, in_grad, rec_grad, bias_grad, dec_grad, dec_bias_grad = pl.pallas_call(
        functools.partial(layer_kernel, dims),
        out_shape=[
            jax.ShapeDtypeStruct((1, 1), f32),
            jax.ShapeDtypeStruct((vocab, width), f32),
            jax.ShapeDtypeStruct((4, width, local_units), f32),
            jax.ShapeDtypeStruct((block, 2 * cols), f32),
            jax.ShapeDtypeStruct((4, local_units), f32),
            jax.ShapeDtypeStruct((dec_rows, vocab), f32),
            jax.ShapeDtypeStruct((1, vocab), f32),
        ],
        in_specs=[vmem] * 9,
        out_specs=[vmem] * 7,
        scratch_shapes=[
            pltpu.VMEM((2, LANES, row_count), jnp.int32),
            pltpu.VMEM((row_count, LANES), jnp.int32),
            pltpu.VMEM((2, block, cols), bf16),
            pltpu.VMEM((2, 8, units, cols), bf16),
            pltpu.VMEM((vocab_rows, LANES), bf16),
            pltpu.VMEM((2, LANES, cols), bf16),
            pltpu.VMEM((2, 1, cols), f32),
            pltpu.VMEM((dec_rows, vocab_pad), bf16),
            pltpu.VMEM((1, vocab_pad), f32),
            pltpu.VMEM((8, units, vocab_pad), bf16),
            pltpu.VMEM((8, steps, rows, units), bf16),
            pltpu.VMEM((steps, 2, half, cols), f32),
            pltpu.VMEM((steps, 2, half, units), f32),
            pltpu.VMEM((steps, vocab_rows, rows), bf16),
            pltpu.VMEM((steps, rows, LANES), bf16),
            pltpu.VMEM((steps, half, LANES), f32),
            pltpu.VMEM((steps, half, LANES), jnp.int32),
            pltpu.VMEM((steps, rows, vocab_pad), bf16),
            pltpu.VMEM((steps, rows, cols), bf16),
            pltpu.VMEM((steps - 1, rows, cols), bf16),
            pltpu.VMEM((2, half, units), f32),
            pltpu.VMEM((2, half, cols), bf16),
            pltpu.VMEM((steps, half, cols), bf16),
            pltpu.VMEM((steps - 1, half, cols), bf16),
            pltpu.VMEM((2, half, cols), bf16),
            pltpu.VMEM((SPLIT, part, 2 * units), f32),
            pltpu.VMEM((steps - 1, SPLIT, 3, part, 2 * units), bf16),
            pltpu.VMEM((steps - 1, SPLIT, 3, part, 2 * units), bf16),
            pltpu.VMEM((1, vocab_pad), f32),
            pltpu.VMEM((2, 1, vocab_pad), f32),
            pltpu.VMEM((2, LANES, cols), f32),
            pltpu.VMEM((4, 2, LANES, cols), f32),
            pltpu.VMEM((4, 2, LANES, cols), bf16),
            pltpu.VMEM((4, 2, LANES, cols), bf16),
            pltpu.VMEM((3, 2, LANES, cols), bf16),
            pltpu.VMEM((3, 2, LANES, cols), bf16),
            pltpu.VMEM((giw_rows, cols), f32),
            pltpu.VMEM((2, giw_rows, units), bf16),
            pltpu.VMEM((2, giw_rows, units), bf16),
            pltpu.VMEM((giw_rows, units), bf16),
            pltpu.VMEM((giw_rows, units), bf16),
            pltpu.VMEM((2, 4, giw_rows, units), bf16),
            pltpu.VMEM((8, emb_rows, LANES), f32),
            pltpu.VMEM((8, emb_rows, LANES), f32),
            pltpu.VMEM((4, emb_rows + 8, LANES), f32),
            pltpu.VMEM((8, emb_rows, LANES), f32),
            pltpu.VMEM((2, 2, dec_rows, vocab_pad), f32),
            pltpu.VMEM((2, dec_rows, vocab_pad), bf16),
            pltpu.VMEM((2, dec_rows, vocab_pad), bf16),
            pltpu.VMEM((dec_rows, vocab_pad), bf16),
            pltpu.VMEM((dec_rows, vocab_pad), bf16),
            sems(1),
            sems(3, PIECES),
            sems(4, PIECES),
            sems(8, PIECES),
            sems(2),
            sems(3),
            sems(7),
            sems(steps, SPLIT, 3),
            sems(steps, SPLIT),
            sems(steps, SPLIT),
            sems(steps, SPLIT),
            sems(steps - 1, SPLIT),
            sems(1),
            sems(steps - 1, SPLIT, 3),
            sems(4, 2, SUB),
            sems(3, 2, SUB),
            sems(5),
            sems(7),
            sems(3),
            sems(7),
            sems(2),
        ],
        compiler_params=pltpu.CompilerParams(
            collective_id=0, has_side_effects=True, vmem_limit_bytes=62 << 20
        ),
    )(
        char_ids.T,
        next_chars.T,
        resets.T,
        embedding,
        in_by_gate,
        by_gate,
        gate_bias,
        dec,
        decoder_bias.reshape(1, vocab),
    )
    return (
        loss.reshape(()),
        emb_grad,
        in_grad.transpose(1, 0, 2),
        rec_grad.reshape(recurrent_weight.shape),
        bias_grad,
        dec_grad.reshape(decoder_weight.shape),
        dec_bias_grad.reshape(vocab),
    )


def on_device(
    char_ids,
    next_chars,
    resets,
    embedding,
    input_weight,
    recurrent_weight,
    gate_bias,
    decoder_weight,
    decoder_bias,
):
    highest = lax.Precision.HIGHEST
    data_count = lax.axis_size("dp")
    row_count, step_count = char_ids.shape
    vocab_size, width_in = embedding.shape
    local_units = input_weight.shape[2]
    gate_cols = 4 * local_units
    tokens_here = row_count * step_count
    tokens_all = tokens_here * data_count
    gathered_rec, gathered_dec = (
        lax.all_gather(recurrent_weight, "dp", axis=0, tiled=True),
        lax.all_gather(decoder_weight, "dp", axis=1, tiled=True),
    )
    hidden_total = gathered_rec.shape[0]
    rec_matrix = gathered_rec.reshape(hidden_total, gate_cols)
    dec_matrix = gathered_dec.reshape(local_units, vocab_size)
    time_ids = char_ids.T
    keep_mask = (1 - resets.T).astype(f32)
    proj_table = jnp.dot(
        embedding, input_weight.reshape(width_in, gate_cols), preferred_element_type=f32
    )
    projected = jnp.take(proj_table, time_ids, axis=0) + gate_bias.reshape(gate_cols)

    def forward_step(state_pair, inputs):
        hidden_loc, cell_state = state_pair
        proj_now, keep_now = inputs
        hidden_full = lax.all_gather(hidden_loc, "mp", axis=1, tiled=True)
        previous = hidden_full * keep_now[:, None].astype(bf16)
        preact = proj_now + jnp.dot(previous, rec_matrix, preferred_element_type=f32)
        gate_vals = preact.reshape(row_count, 4, local_units)
        in_gate = jax.nn.sigmoid(gate_vals[:, 0])
        forget_gate = jax.nn.sigmoid(gate_vals[:, 1])
        cell_gate = jnp.tanh(gate_vals[:, 2])
        out_gate = jax.nn.sigmoid(gate_vals[:, 3])
        new_cell = forget_gate * cell_state * keep_now[:, None] + in_gate * cell_gate
        new_hidden = (out_gate * jnp.tanh(new_cell)).astype(bf16)
        return ((new_hidden, new_cell), (previous, preact, new_cell, new_hidden))

    first_state = (
        jnp.zeros((row_count, local_units), bf16),
        jnp.zeros((row_count, local_units), f32),
    )
    _, (prevs, preacts, cells, hiddens) = lax.scan(
        forward_step, first_state, (projected, keep_mask)
    )
    flat_hidden = hiddens.reshape(tokens_here, local_units)
    partial_value = jnp.dot(flat_hidden, dec_matrix, preferred_element_type=f32)
    flat_targets = next_chars.T.reshape(tokens_here)
    logit_rows = lax.psum(partial_value, "mp")
    shifted_in = logit_rows + decoder_bias
    row_max = jnp.max(shifted_in, axis=1)
    exp_total = jnp.sum(jnp.exp(shifted_in - row_max[:, None]), axis=1)
    log_total = row_max + jnp.log(exp_total)
    softmax_out = jnp.exp(shifted_in - log_total[:, None])
    onehot = (flat_targets[:, None] == jnp.arange(vocab_size, dtype=jnp.int32)[None, :]).astype(f32)
    picked = jnp.sum(shifted_in * onehot, axis=1)
    grad_rows = ((softmax_out - onehot) / tokens_all).astype(bf16)
    local_loss = jnp.sum(log_total - picked) / tokens_all
    loss_part = jnp.where(lax.axis_index("mp") == 0, local_loss, jnp.zeros((), f32))
    out_grads = jnp.dot(grad_rows, dec_matrix.T, preferred_element_type=f32).reshape(
        step_count, row_count, local_units
    )
    dec_bias_part = jnp.sum(grad_rows.astype(f32), axis=0)
    columns = flat_hidden
    dec_grad = lax.psum_scatter(
        lax.dot_general(columns, grad_rows, (((0,), (0,)), ((), ())), preferred_element_type=f32),
        "dp",
        scatter_dimension=0,
        tiled=True,
    ).reshape(decoder_weight.shape)
    prev_cells = (
        jnp.concatenate([jnp.zeros((1, row_count, local_units), f32), cells[:-1]], axis=0)
        * keep_mask[:, :, None]
    )

    def backward_step(state_pair, inputs):
        carry_hidden, carry_cell = state_pair
        preact, cell_state, prev_cell, hidden_out, keep_now = inputs
        gate_vals = preact.reshape(row_count, 4, local_units)
        in_gate = jax.nn.sigmoid(gate_vals[:, 0])
        forget_gate = jax.nn.sigmoid(gate_vals[:, 1])
        cell_gate = jnp.tanh(gate_vals[:, 2])
        out_gate = jax.nn.sigmoid(gate_vals[:, 3])
        hidden_grad = hidden_out + carry_hidden
        squash = jnp.tanh(cell_state)
        cell_grad = hidden_grad * out_gate * (1.0 - squash * squash) + carry_cell
        grad_in = cell_grad * cell_gate * in_gate * (1.0 - in_gate)
        grad_forget = cell_grad * prev_cell * forget_gate * (1.0 - forget_gate)
        grad_cand = cell_grad * in_gate * (1.0 - cell_gate * cell_gate)
        grad_out = hidden_grad * squash * out_gate * (1.0 - out_gate)
        preact_grad = (
            jnp.stack([grad_in, grad_forget, grad_cand, grad_out], axis=1)
            .reshape(row_count, gate_cols)
            .astype(bf16)
        )
        back_term = lax.dot_general(
            preact_grad, rec_matrix, (((1,), (1,)), ((), ())), preferred_element_type=f32
        )
        next_hidden = (
            lax.psum_scatter(back_term, "mp", scatter_dimension=1, tiled=True) * keep_now[:, None]
        )
        next_cell = cell_grad * forget_gate * keep_now[:, None]
        return ((next_hidden, next_cell), preact_grad)

    zero_rows = jnp.zeros((row_count, local_units), f32)
    _, preact_grads = lax.scan(
        backward_step,
        (zero_rows, zero_rows),
        (preacts, cells, prev_cells, out_grads, keep_mask),
        reverse=True,
    )
    flat_prev = prevs.reshape(tokens_here, hidden_total)
    flat_pgrad = preact_grads.reshape(tokens_here, gate_cols)
    columns = flat_prev
    rec_grad = lax.psum_scatter(
        lax.dot_general(columns, flat_pgrad, (((0,), (0,)), ((), ())), preferred_element_type=f32),
        "dp",
        scatter_dimension=0,
        tiled=True,
    ).reshape(recurrent_weight.shape)
    onehot_ids = (
        time_ids.reshape(tokens_here)[:, None] == jnp.arange(vocab_size, dtype=jnp.int32)[None, :]
    ).astype(bf16)
    table_part = lax.dot_general(
        onehot_ids, flat_pgrad, (((0,), (0,)), ((), ())), preferred_element_type=f32
    )
    table_sum, dec_bias_grad, loss_data = lax.psum((table_part, dec_bias_part, loss_part), "dp")
    in_grad = jnp.dot(embedding.astype(f32).T, table_sum, precision=highest).reshape(
        width_in, 4, local_units
    )
    bias_grad = jnp.sum(table_sum, axis=0).reshape(4, local_units)
    emb_part = lax.dot_general(
        table_sum,
        input_weight.reshape(width_in, gate_cols).astype(f32),
        (((1,), (1,)), ((), ())),
        precision=highest,
    )
    emb_grad, loss = lax.psum((emb_part, loss_data), "mp")
    return (loss, emb_grad, in_grad, rec_grad, bias_grad, dec_grad, dec_bias_grad)


def solution(mesh):
    in_specs = (
        P("dp", None),
        P("dp", None),
        P("dp", None),
        P(),
        P(None, None, "mp"),
        P("dp", None, "mp"),
        P(None, "mp"),
        P("mp", "dp", None, None),
        P(),
    )
    out_specs = (
        P(),
        P(),
        P(None, None, "mp"),
        P("dp", None, "mp"),
        P(None, "mp"),
        P("mp", "dp", None, None),
        P(),
    )
    fits = (mesh.shape["dp"], mesh.shape["mp"]) == (8, 4)
    return jax.shard_map(
        grouped if fits else on_device,
        mesh=mesh,
        in_specs=in_specs,
        out_specs=out_specs,
        check_vma=False,
    )
```

time: 285 us -> 230 us (0.81)
  Pallas kernels: 259 us -> 214 us
  local copies, waits for them, and re-layouts: 21.2 us -> 13 us
    pallas_call x1, Pallas kernels: 259 us -> 214 us  [grouped(): pl.pallas_call(functools.partial(layer_kernel, dims), out_shape=[jax.Shap...]
    unnamed x6 -> x16, local copies, waits for them, and re-layouts: 0.01 us -> 8.72 us
    slice x5 -> x0, local copies, waits for them, and re-layouts: 6.3 us -> none  [the longest x1 1.58 us: grouped(): emb_grad = out_emb.reshape(8 * emb_rows, LANES)[:vocab, :width]]
    reshape x11 -> x1, local copies, waits for them, and re-layouts: 9.92 us -> 3.67 us  [grouped(): rec_grad.reshape(recurrent_weight.shape)]
    pad x4 -> x0, local copies, waits for them, and re-layouts: 3.48 us -> none  [the longest x1 1.42 us: grouped(): jnp.pad(decoder_weight.reshape(dec_rows, vocab), ((0, 0), (0, vocab_pad -...]
where the time goes in v2:
time: 230 us; the launch traced here: 229 us
  Pallas kernels  214 us (93%)
  local copies, waits for them, and re-layouts  13 us (6%)
  between operations  2.44 us (1%)
    pallas_call x1, Pallas kernels, grouped(): pl.pallas_call(functools.partial(layer_kernel, dims), out_shape=[jax.Shap...  214 us
    unnamed x16, local copies, waits for them, and re-layouts  8.72 us

profile of v2, /device:TPU:1, one launch (start us, length us, event | category | flops | bytes accessed | tf_op | source)
XLA Modules:
  0.0 229.5 jit_solution(13470030765043409173)
XLA Ops:
  0.6 0.0 copy-start.3
  0.6 1.8 copy.22
  2.5 2.4 %copy.21 = bf16[256,4,512]{2,0,1:T(8,128)(2,1)} copy(bf16[256,4,512]{2,1,0:T(4,128)(2,1)} %param.14) | data formatting | bytes 2097152 | tf_op args[5]
  4.9 0.0 copy-done.3
  4.9 0.6 reshape.33.decb_ref
  5.4 213.5 %shard_map.144 = (f32[1,1]{1,0:T(1,128)}, f32[275,100]{1,0:T(8,128)}, f32[4,100,512]{2,1,0:T(8,128)}, f32[256,2048]{1,0:T(8,128)}, f32[4,512]{1,0:T(4,128)}, /*index=5*/f32[64,275]{1,0:T(8,128)}, f32[1,275]{1,0:T(1,128)}) custom-call(s32[6,128]{1,0:T(8,128)} %bitcast.18, s32[6,128]{1,0:T(8,128)} %bitcast.19, s32[6,128]{1,0:T(8,128)} %bitcast.20, ...), custom_call_target="tpu_custom_call" | custom-call | tf_op jit(solution)/shard_map/pallas_call | solution.py:897
  219.0 2.6 %copy.18 = f32[100,4,512]{2,1,0:T(4,128)} copy(f32[100,4,512]{2,0,1:T(8,128)} %bitcast.15) | data formatting | bytes 1638400
  221.5 0.0 copy-start.4
  221.5 0.0 copy-start
  221.5 0.0 copy-start.2
  221.5 0.0 copy-start.1
  221.5 3.7 %reshape.35 = f32[256,4,512]{2,1,0:T(4,128)} reshape(f32[256,2048]{1,0:T(8,128)} %get-tuple-element.17) | data formatting | bytes 4194304 | tf_op jit(solution)/shard_map/reshape | solution.py:1002
  225.2 0.0 copy-done.4
  225.2 0.6 reduce
  226.4 0.0 copy-done
  226.5 0.7 copy.28
  227.1 0.0 copy-done.2
  227.1 0.6 copy.29
  227.7 0.0 copy-done.1
  227.7 0.6 copy.30
Async XLA Ops:
  0.6 4.2 %copy-start.3 = (f32[275]{0:T(512)S(1)}, f32[275]{0:T(512)}, u32[]{:S(2)}) copy-start(f32[275]{0:T(512)} %param.17) | copy-start | bytes 3304
  221.5 3.7 %copy-start.4 = (f32[1,275]{1,0:T(1,128)S(1)}, f32[1,275]{1,0:T(1,128)}, u32[]{:S(2)}) copy-start(f32[1,275]{1,0:T(1,128)} %get-tuple-element.20) | copy-start | bytes 3304
  221.5 4.9 %copy-start = (f32[275,100]{1,0:T(8,128)S(1)}, f32[275,100]{1,0:T(8,128)}, u32[]{:S(2)}) copy-start(f32[275,100]{1,0:T(8,128)} %get-tuple-element.36) | copy-start | bytes 330004
  221.5 5.6 %copy-start.2 = (f32[4,512]{1,0:T(4,128)S(1)}, f32[4,512]{1,0:T(4,128)}, u32[]{:S(2)}) copy-start(f32[4,512]{1,0:T(4,128)} %get-tuple-element.39) | copy-start | bytes 24580
  221.5 6.2 %copy-start.1 = (f32[64,275]{1,0:T(8,128)S(1)}, f32[64,275]{1,0:T(8,128)}, u32[]{:S(2)}) copy-start(f32[64,275]{1,0:T(8,128)} %get-tuple-element.19) | copy-start | bytes 211204

commit v3 on v2

--- a/solution.py
+++ b/solution.py
@@ -18,7 +18,9 @@
 COLUMN = (4, 6, 2)
 SPLIT = 2
 PIECES = 8
-SUB = 2
+LAG = 2
+EARLY = 3
+SUB = 4
 
 
 def turn(value, flips):
@@ -58,6 +60,15 @@
     out_gb,
     out_dec,
     out_decb,
+    rec_in,
+    iw_in,
+    rec_final,
+    iw_final,
+    gb_final,
+    loss_final,
+    decb_final,
+    dec_final,
+    emb_final,
     ids_rows,
     ids_cols,
     rec_halves,
@@ -109,6 +120,8 @@
     dec_x_in,
     dec_z_out,
     dec_z_in,
+    in_sem,
+    out_sem,
     ids_sem,
     wz_sem,
     wx_sem,
@@ -161,20 +174,32 @@
             device_id_type=MESH,
         )
 
+    sizes = [block // PIECES] * (PIECES - 1) + [block // PIECES // 2] * 2
+    pieces = [(sum(sizes[:p]), size) for p, size in enumerate(sizes)]
+    rec_loads = [
+        pltpu.make_async_copy(
+            rec_ref.at[pl.ds(first, size)], rec_in.at[pl.ds(first, size)], in_sem.at[p]
+        )
+        for p, (first, size) in enumerate(pieces)
+    ]
+    iw_load = pltpu.make_async_copy(iw_ref, iw_in, in_sem.at[PIECES + 1])
+    for each in rec_loads + [iw_load]:
+        each.start()
+
     barrier = pltpu.get_barrier_semaphore()
     for flips in PEERS:
         pl.semaphore_signal(barrier, inc=1, device_id=device(flips), device_id_type=MESH)
     pl.semaphore_wait(barrier, len(PEERS))
 
-    piece = block // PIECES
 
     def weight_rows(index, p):
-        first = p * piece
+        first, size = pieces[p]
         side, inside = first // LANES, first % LANES
         return weights.at[
             core,
             side * 4 + lax.div(index, 2),
-            pl.ds(pl.multiple_of(lax.rem(index, 2) * LANES + inside, piece), piece),
+            :,
+            pl.ds(pl.multiple_of(lax.rem(index, 2) * LANES + inside, size), size),
         ]
 
     def weight_core(index, at, p):
@@ -188,7 +213,7 @@
         flips = COLUMN[k]
         half = turn(z_low, (flips & 2) // 2)
         return copy(
-            rec_halves.at[half, pl.ds(p * piece, piece)], weight_rows(d, p), wz_sem, (k, p), (flips, 0)
+            rec_halves.at[half, :, pl.ds(*pieces[p])], weight_rows(d, p), wz_sem, (k, p), (flips, 0)
         )
 
     def weight_z_in(k, p):
@@ -198,7 +223,7 @@
     def weight_x(k, p):
         if k == 3:
             return copy(
-                rec_halves.at[z_low, pl.ds(p * piece, piece)],
+                rec_halves.at[z_low, :, pl.ds(*pieces[p])],
                 weight_rows(d, p),
                 wx_sem,
                 (k, p),
@@ -213,7 +238,7 @@
         return copy(spot, spot, wx_sem, (k, p), (1, 0))
 
     runs = units // LANES
-    width = iw_ref.shape[1]
+    width = iw_ref.shape[0]
     dec_rows = dec_ref.shape[0]
     vocab_rows = emb_pad.shape[0]
 
@@ -226,17 +251,23 @@
     ids_rows[z_low, 16 : 16 + steps] = resets_ref[...]
     ids_copy = copy(ids_rows.at[z_low], ids_rows.at[z_low], ids_sem, (0,), (2, 0))
     ids_copy.start()
-    for p in range(PIECES):
-        here = slice(p * piece, (p + 1) * piece)
+
+    def weight_start(p):
+        for k in range(3):
+            weight_z(k, p).start()
+        weight_x(3, p).start()
+
+    for p, (first, size) in enumerate(pieces):
+        here = slice(first, first + size)
+        rec_loads[p].wait()
         for gate in range(4):
             for run in range(runs):
                 for side in range(2):
                     at = (run * 2 + side) * LANES
-                    to = gate * units + run * LANES
-                    rec_halves[side, here, to : to + LANES] = rec_ref[gate, here, at : at + LANES]
-        for k in range(3):
-            weight_z(k, p).start()
-        weight_x(3, p).start()
+                    to = run * LANES
+                    rec_halves[side, gate, here, to : to + LANES] = rec_in[here, gate, at : at + LANES]
+        if p < EARLY:
+            weight_start(p)
         if p == 0:
             dec_pad[...] = jnp.zeros_like(dec_pad)
             dec_pad[:, :vocab] = dec_ref[...]
@@ -250,8 +281,22 @@
             weight_z_in(k, p).wait_recv()
             weight_x(k, p).start()
             weight_core(block_of(1 + k), 1 + k, p).start()
-        if p:
-            weight_over_x(p - 1)
+        if p >= LAG:
+            weight_over_x(p - LAG)
+
+    def weights_from_core(which):
+        for p in which:
+            for at in range(8):
+                index = block_of(at)
+                first, size = pieces[p]
+                inside = first % LANES
+                spot = weights.at[
+                    1 - core,
+                    first // LANES * 4 + lax.div(index, 2),
+                    :,
+                    pl.ds(pl.multiple_of(lax.rem(index, 2) * LANES + inside, size), size),
+                ]
+                copy(spot, spot, wc_sem, (at, p), (0, 1)).wait_recv()
 
     def weight_over_x(p):
         for k in (3, 0, 1, 2):
@@ -259,8 +304,8 @@
             at = 4 if k == 3 else 5 + k
             weight_core(block_of(at), at, p).start()
 
-    for p in range(PIECES):
-        weight_rows(d, p)[...] = rec_halves[z_low, pl.ds(p * piece, piece)]
+    for p in range(PIECES + 1):
+        weight_rows(d, p)[...] = rec_halves[z_low, :, pl.ds(*pieces[p])]
         weight_core(block_of(0), 0, p).start()
     dec_spot(0)[...] = dec_pad[...]
     emb_pad[...] = jnp.zeros_like(emb_pad)
@@ -268,6 +313,7 @@
     ones_at = lax.broadcasted_iota(jnp.int32, emb_pad.shape, 1) == width
     emb_pad[...] = jnp.where(ones_at, 1.0, emb_pad[...].astype(f32)).astype(bf16)
     iw_pads[core] = jnp.zeros(iw_pads.shape[1:], bf16)
+    iw_load.wait()
 
     def half_lanes(run):
         return pl.ds(pl.multiple_of((run * 2 + z_low) * LANES, LANES), LANES)
@@ -275,7 +321,7 @@
     for gate in range(4):
         for run in range(runs):
             to = gate * units + run * LANES
-            iw_pads[core, :width, to : to + LANES] = iw_ref[gate, :, half_lanes(run)]
+            iw_pads[core, :width, to : to + LANES] = iw_in[:, gate, half_lanes(run)]
             gb_pads[core, :, to : to + LANES] = gb_ref[gate : gate + 1, half_lanes(run)]
     iw_copies = [
         copy(ref.at[core], ref.at[core], iw_sem, (k,), (0, 1))
@@ -284,7 +330,7 @@
     for each in iw_copies:
         each.start()
     decb_pad[...] = jnp.full(decb_pad.shape, -1e30, f32)
-    decb_pad[:, :vocab] = decb_ref[...]
+    decb_pad[0, :vocab] = decb_ref[...]
     ids_copy.wait_recv()
     ids_cols[...] = ids_rows[core].T
     vocab_iota = lax.broadcasted_iota(jnp.int32, (vocab_rows, rows), 0)
@@ -335,13 +381,13 @@
         if added is not None:
             keep = keeps[t, here, :1]
         for c in range(2):
-            preact = gates[t, c, here]
+            preact = [gates[t, c, here, k * units : (k + 1) * units] for k in range(4)]
             if added is not None:
-                preact = preact + keep * added[c]
-            in_gate = jax.nn.sigmoid(preact[:, :units])
-            forget = jax.nn.sigmoid(preact[:, units : 2 * units])
-            candidate = jnp.tanh(preact[:, 2 * units : 3 * units])
-            out_gate = jax.nn.sigmoid(preact[:, 3 * units :])
+                preact = [preact[k] + keep * added[c][k] for k in range(4)]
+            in_gate = jax.nn.sigmoid(preact[0])
+            forget = jax.nn.sigmoid(preact[1])
+            candidate = jnp.tanh(preact[2])
+            out_gate = jax.nn.sigmoid(preact[3])
             cell = in_gate * candidate
             if added is not None:
                 cell = forget * keep * cells[t - 1, c, here] + cell
@@ -354,9 +400,18 @@
         for j in (2, 0, 1):
             hidden_copy(t, s, j).start()
 
+    def add_slot(total, t, s, at):
+        some = hid[at, t, wide(s)]
+        for c in range(2):
+            for gate in range(4):
+                more = dot(some, weights[c, at, gate])
+                total[c][gate] = more if total[c][gate] is None else total[c][gate] + more
+
     for s in range(SPLIT):
         cell_step(0, s, None)
 
+    for p in range(EARLY, PIECES + 1):
+        weight_start(p)
     weight_round(0)
     project(1)
     project(2)
@@ -381,45 +436,37 @@
         each.start()
     weight_round(4)
     weight_round(5)
+    weights_from_core(range(PIECES // 2))
+    for s in range(SPLIT):
+        for j in range(3):
+            hidden_in(0, s, j).wait_recv()
+        total = [[None] * 4, [None] * 4]
+        for at in range(4):
+            add_slot(total, 0, s, at)
+        for c in range(2):
+            for gate in range(4):
+                lanes = slice(gate * units, (gate + 1) * units)
+                gates[1, c, span(s), lanes] += keeps[1, span(s), :1] * total[c][gate]
+    for p in range(6, PIECES + 1):
+        weight_round(p)
+    for p in range(PIECES + 1 - LAG, PIECES + 1):
+        weight_over_x(p)
+    weights_from_core(range(PIECES // 2, PIECES + 1))
+
     dec_relays = []
     for j in range(3):
         spot = dec_all.at[slot(CHIPS[j])]
         copy(spot, spot, decr_sem, (j,), CHIPS[j]).wait_recv()
-        each = copy(spot, spot, decr_sem, (4 + j,), (0, 1))
-        each.start()
-        dec_relays.append(each)
-    for p in range(6, PIECES):
-        weight_round(p)
-    spot = dec_all.at[slot((0, 1))]
-    copy(spot, spot, decr_sem, (3,), (0, 1)).wait_recv()
-    for j in range(3):
-        spot = dec_all.at[slot((CHIPS[j][0], CHIPS[j][1] + 1))]
-        copy(spot, spot, decr_sem, (4 + j,), (0, 1)).wait_recv()
-    weight_over_x(PIECES - 1)
-    for p in range(PIECES):
-        for at in range(8):
-            spot = weights.at[
-                1 - core,
-                (p * piece // LANES) * 4 + lax.div(block_of(at), 2),
-                pl.ds(
-                    pl.multiple_of(
-                        lax.rem(block_of(at), 2) * LANES + p * piece % LANES, piece
-                    ),
-                    piece,
-                ),
-            ]
-            copy(spot, spot, wc_sem, (at, p), (0, 1)).wait_recv()
+        dec_relays.append(copy(spot, spot, decr_sem, (4 + j,), (0, 1)))
+        dec_relays[-1].start()
 
     def add_chip(total, t, s, flips):
         first = turn(z_low, flips[0] // 2) * 4 + turn(y_at, flips[1] // 2) * 2
         for k in range(2):
-            some = hid[first + k, t, wide(s)]
-            for c in range(2):
-                more = dot(some, weights[c, first + k])
-                total[c] = more if total[c] is None else total[c] + more
+            add_slot(total, t, s, first + k)
 
     def gather_hidden(t, s):
-        total = [None, None]
+        total = [[None] * 4, [None] * 4]
         add_chip(total, t, s, (0, 0))
         for j in range(3):
             hidden_in(t, s, j).wait_recv()
@@ -459,7 +506,20 @@
             decode(t - 1, s)
         return 0
 
-    lax.fori_loop(1, steps, forward, 0)
+    for s in range(SPLIT):
+        total = [[None] * 4, [None] * 4]
+        for at in range(4, 8):
+            add_slot(total, 0, s, at)
+        cell_step(1, s, total)
+        hidden_core(0, s).start()
+    spot = dec_all.at[slot((0, 1))]
+    copy(spot, spot, decr_sem, (3,), (0, 1)).wait_recv()
+    for j in range(3):
+        spot = dec_all.at[slot((CHIPS[j][0], CHIPS[j][1] + 1))]
+        copy(spot, spot, decr_sem, (4 + j,), (0, 1)).wait_recv()
+    for s in range(SPLIT):
+        decode(0, s)
+    lax.fori_loop(2, steps, forward, 0)
 
     def pg_copy(t, s):
         return copy(pg_out.at[t, span(s)], pgs.at[t, wide(s)], pg_sem, (t, s), (0, 1))
@@ -522,9 +582,12 @@
             flips = CHIPS[j] if j < 3 else (0, 0)
             first = turn(z_low, flips[0] // 2) * 4 + turn(y_at, flips[1] // 2) * 2
             for k in range(2):
-                part_sum = dot_t(pgm_now[0, here], weights[0, first + k]) + dot_t(
-                    pgm_now[1, here], weights[1, first + k]
-                )
+                part_sum = None
+                for c in range(2):
+                    for gate in range(4):
+                        grad = pgm_now[c, here, gate * units : (gate + 1) * units]
+                        more = dot(grad, weights[c, first + k, gate])
+                        part_sum = more if part_sum is None else part_sum + more
                 lanes = slice(k * units, (k + 1) * units)
                 if j < 3:
                     chip_out[t - 1, s, j, :, lanes] = part_sum.astype(bf16)
@@ -541,6 +604,20 @@
         return total
 
     last = steps - 1
+
+    for p in range(PIECES + 1):
+        for at in range(8):
+            weight_core(block_of(at), at, p).wait_send()
+        for k in range(4):
+            weight_x(k, p).wait_send()
+
+    def turn_over(at, _):
+        for c in range(2):
+            for gate in range(4):
+                weights[c, at, gate] = weights[c, at, gate].T
+        return 0
+
+    lax.fori_loop(0, 8, turn_over, 0)
     for s in range(SPLIT):
         for j in range(3):
             hidden_in(last, s, j).wait_recv()
@@ -550,12 +627,56 @@
         spread(last, s)
         share(last, s, False)
 
+    def other_rows(s):
+        return pl.ds(pl.multiple_of((1 - core) * half + s * part, part), part)
+
+    def dsum_x():
+        return copy(dec_x_out, dec_x_in, dsum_sem, (0,), (1, 0))
+
+    def dsum_z(k):
+        return copy(dec_z_out, dec_z_in, dsum_sem, (k,), (4, 0))
+
+    def small_copy():
+        return copy(small_pair.at[core], small_pair.at[core], small_sem, (0,), (0, 1))
+
+    def decoder_grad():
+        for t in range(steps):
+            for s in range(SPLIT):
+                hidden_core_in(t, s).wait_recv()
+                spot = logit_grads.at[t, other_rows(s)]
+                copy(spot, spot, lg_sem, (t, s), (0, 1)).wait_recv()
+        small_pair[core] = small_acc[...]
+        small_copy().start()
+        dec_part[...] = t_dot(
+            hid[own].reshape(steps * rows, units),
+            logit_grads[...].reshape(steps * rows, vocab_pad),
+        ).reshape(2, 2, dec_rows, vocab_pad)
+        for k in range(2):
+            dec_x_out[k] = dec_part[k, 1 - x_at].astype(bf16)
+        dsum_x().start()
+
+    def decoder_grad_z():
+        dsum_x().wait_recv()
+        dec_z_out[...] = (
+            dec_part[1 - z_high, x_at] + dec_x_in[1 - z_high].astype(f32)
+        ).astype(bf16)
+        dsum_z(1).start()
+
     def backward(i, _):
         t = last - i
         for s in range(SPLIT):
             cell_back(t, s, carried_in(t, s), False)
             spread(t, s)
             share(t, s, False)
+
+        @pl.when(i == 2)
+        def _():
+            decoder_grad()
+
+        @pl.when(i == 3)
+        def _():
+            decoder_grad_z()
+
         return 0
 
     lax.fori_loop(1, last, backward, 0)
@@ -578,26 +699,15 @@
 
     used = (steps - 1) * rows
 
-    def from_core(t, first):
+    def from_core(t, _):
         for s in range(SPLIT):
-            hidden_core_in(t, s).wait_recv()
-            rows_there = pl.ds(pl.multiple_of((1 - core) * half + s * part, part), part)
-            spot = logit_grads.at[t, rows_there]
-            copy(spot, spot, lg_sem, (t, s), (0, 1)).wait_recv()
-            spot = pgs.at[t, rows_there]
+            spot = pgs.at[t, other_rows(s)]
             copy(spot, spot, pg_sem, (t, s), (0, 1)).wait_recv()
-            if not first:
-                spot = pgm.at[t - 1, rows_there]
-                copy(spot, spot, pgm_sem, (t - 1, s), (0, 1)).wait_recv()
-
-    def all_from_core(t, _):
-        from_core(t, False)
+            spot = pgm.at[t - 1, other_rows(s)]
+            copy(spot, spot, pgm_sem, (t - 1, s), (0, 1)).wait_recv()
         return 0
 
-    lax.fori_loop(1, steps, all_from_core, 0)
-    hidden_0 = [hidden_core_in(0, s) for s in range(SPLIT)]
-    for each in hidden_0:
-        each.wait_recv()
+    lax.fori_loop(1, steps, from_core, 0)
 
     def weight_grad(k, side):
         at = side * 4 + turn(z_at, far[k])
@@ -609,11 +719,16 @@
 
     order = [(k, side, sub) for k in range(4) for side in range(2) for sub in range(SUB)]
 
-    def send_x(first, last):
-        for spot in order[first:last]:
-            x_copy(*spot).start()
+    def send_eighth(*which):
+        for at in which:
+            for k in range(SUB // 2):
+                x_copy(*order[at * (SUB // 2) + k]).start()
 
     def pass_z(at):
+        for k in range(SUB // 2):
+            pass_piece(at * (SUB // 2) + k)
+
+    def pass_piece(at):
         k, side, sub = order[at]
         here = pl.ds(sub * piece_rows, piece_rows)
         x_copy(k, side, sub).wait_recv()
@@ -622,32 +737,22 @@
             acc[k, side, here] = total
             return
         z_out[k, side, here] = total.astype(bf16)
-        if at in range(2, 4 * SUB):
-            z_copy(*order[at - 2]).wait_send()
+        if at in range(SUB, 4 * SUB):
+            z_copy(*order[at - SUB]).wait_send()
         z_copy(k, side, sub).start()
 
     weight_grad(0, 0)
-    send_x(0, SUB)
+    send_eighth(0, 1)
     weight_grad(0, 1)
-    send_x(SUB, 2 * SUB)
-    weight_grad(1, 0)
-    weight_grad(1, 1)
+    send_eighth(2, 3)
     pass_z(0)
 
     for s in range(SPLIT):
         cell_back(0, s, carried_in(0, s), True)
         share(0, s, True)
-    small_pair[core] = small_acc[...]
-    small_copy = copy(small_pair.at[core], small_pair.at[core], small_sem, (0,), (0, 1))
-    small_copy.start()
     for s in range(SPLIT):
-        rows_there = pl.ds(pl.multiple_of((1 - core) * half + s * part, part), part)
-        spot = logit_grads.at[0, rows_there]
-        copy(spot, spot, lg_sem, (0, s), (0, 1)).wait_recv()
-        spot = pgs.at[0, rows_there]
+        spot = pgs.at[0, other_rows(s)]
         copy(spot, spot, pg_sem, (0, s), (0, 1)).wait_recv()
-    spot = small_pair.at[1 - core]
-    copy(spot, spot, small_sem, (0,), (0, 1)).wait_recv()
     tokens = steps * rows
     giw_rows = giw_acc.shape[0]
     giw_acc[...] = t_dot(
@@ -658,15 +763,10 @@
         giw_out[k] = giw_acc[:, pl.ds(at, units)].astype(bf16)
     giw_x = copy(giw_out, giw_x_in, giw_sem, (0,), (1, 0))
     giw_x.start()
-    dec_part[...] = t_dot(
-        hid[own].reshape(tokens, units), logit_grads[...].reshape(tokens, vocab_pad)
-    ).reshape(2, 2, dec_rows, vocab_pad)
-    for k in range(2):
-        dec_x_out[k] = dec_part[k, 1 - x_at].astype(bf16)
-    dsum_x = copy(dec_x_out, dec_x_in, dsum_sem, (0,), (1, 0))
-    dsum_x.start()
-    send_x(2 * SUB, 3 * SUB)
     pass_z(1)
+    weight_grad(1, 0)
+    weight_grad(2, 0)
+    send_eighth(4, 8)
 
     emb_rows = emb_full.shape[1]
     by_char = jnp.zeros((vocab_rows, 2 * LANES), f32)
@@ -684,7 +784,9 @@
         each.start()
     emb_in[own] = emb_part[own]
     pass_z(2)
-    send_x(3 * SUB, 4 * SUB)
+    weight_grad(1, 1)
+    weight_grad(2, 1)
+    send_eighth(5, 9)
 
     giw_x.wait_recv()
     for k in range(2):
@@ -695,12 +797,6 @@
     ].astype(bf16)
     giw_z = copy(giw_z_out, giw_z_in, giw_sem, (1,), (4, 0))
     giw_z.start()
-    dsum_x.wait_recv()
-    dec_z_out[...] = (
-        dec_part[1 - z_high, x_at] + dec_x_in[1 - z_high].astype(f32)
-    ).astype(bf16)
-    dsum_z = copy(dec_z_out, dec_z_in, dsum_sem, (1,), (4, 0))
-    dsum_z.start()
     for j, flips in enumerate(GROUP):
         spot = emb_in.at[slot(flips)]
         copy(spot, spot, emb_sem, (j,), flips).wait_recv()
@@ -712,6 +808,8 @@
         return turn(z_high, flips // 4) * 2 + turn(x_at, flips % 2)
 
     emb_sums[place(0), :emb_rows] = total
+    spot = small_pair.at[1 - core]
+    copy(spot, spot, small_sem, (0,), (0, 1)).wait_recv()
     smalls = small_pair[0] + small_pair[1]
     for k in range(vocab_pad // LANES):
         emb_sums[place(0), emb_rows + k : emb_rows + k + 1] = smalls[
@@ -722,11 +820,11 @@
     for each in emb2:
         each.start()
     pass_z(3)
-    weight_grad(2, 0)
-    weight_grad(2, 1)
-    send_x(4 * SUB, 5 * SUB)
     weight_grad(3, 0)
     weight_grad(3, 1)
+    pass_z(4)
+    pass_z(8)
+    send_eighth(6, 10)
 
     giw_z.wait_recv()
     gate_at = x_at * 2 + z_high
@@ -736,8 +834,9 @@
     spot = giw_full.at[z_low, gate_at]
     giw_back_z = copy(spot, spot, giw_sem, (2,), (4, 0))
     giw_back_z.start()
-    pass_z(4)
-    send_x(5 * SUB, 6 * SUB)
+    pass_z(5)
+    pass_z(9)
+    send_eighth(7, 11, 12, 13)
     for j, flips in enumerate(OTHERS):
         spot = emb_sums.at[place(flips)]
         copy(spot, spot, emb2_sem, (j,), (flips, 0)).wait_recv()
@@ -749,32 +848,73 @@
         each.start()
     for k in range(vocab_pad // LANES):
         lanes = slice(k * LANES, min(vocab, (k + 1) * LANES))
-        out_decb[:, lanes] = sums[emb_rows + k : emb_rows + k + 1, : lanes.stop - lanes.start]
+        decb_final[:, lanes] = sums[emb_rows + k : emb_rows + k + 1, : lanes.stop - lanes.start]
     k = vocab_pad // LANES - 1
-    out_loss[...] = sums[emb_rows + k : emb_rows + k + 1, LANES - 1 :]
-    pass_z(5)
+    loss_final[...] = sums[emb_rows + k : emb_rows + k + 1, LANES - 1 :]
     spot = giw_full.at[z_low, x_at * 2 + 1 - z_high]
     copy(spot, spot, giw_sem, (2,), (4, 0)).wait_recv()
     spot = giw_full.at[z_low, pl.ds(x_at * 2, 2)]
     giw_back_x = copy(spot, spot, giw_sem, (3,), (1, 0))
     giw_back_x.start()
-    send_x(6 * SUB, 8 * SUB)
+    send_eighth(14, 15)
     pass_z(6)
-    dsum_z.wait_recv()
+    pass_z(10)
+    dsum_z(1).wait_recv()
     total = dec_part[z_high, x_at] + dec_x_in[z_high].astype(f32) + dec_z_in[...].astype(f32)
-    out_dec[...] = total[:, :vocab]
+    dec_final[...] = total[:, :vocab]
     spot = giw_full.at[z_low, pl.ds((1 - x_at) * 2, 2)]
     copy(spot, spot, giw_sem, (3,), (1, 0)).wait_recv()
     spot = giw_full.at[z_low]
     giw_side = copy(spot, spot, giw_sem, (4,), (2, 0))
     giw_side.start()
     pass_z(7)
+    pass_z(11)
+    ids_copy.wait_send()
+    dec_z.wait_send()
+    for each in dec_x + dec_sends + dec_relays + iw_copies + [small_copy(), dsum_x(), dsum_z(1)]:
+        each.wait_send()
+    for p in range(PIECES + 1):
+        for k in range(3):
+            weight_z(k, p).wait_send()
+
+    def sent(t, _):
+        for s in range(SPLIT):
+            for j in range(3):
+                hidden_copy(t, s, j).wait_send()
+            hidden_core(t, s).wait_send()
+            lg_copy(t, s).wait_send()
+            pg_copy(t, s).wait_send()
+        return 0
+
+    lax.fori_loop(0, steps, sent, 0)
+
+    def sent_back(t, _):
+        for s in range(SPLIT):
+            pgm_copy(t, s).wait_send()
+            for j in range(3):
+                chip_copy(t, s, j).wait_send()
+        return 0
+
+    lax.fori_loop(1, steps, sent_back, 0)
     for j, flips in enumerate(GROUP):
         spot = emb_full.at[slot(flips)]
         copy(spot, spot, emb3_sem, (j,), flips).wait_recv()
-    out_emb[...] = emb_full[...].reshape(vocab_rows, LANES)[:vocab, :width]
-    for at in range(4 * SUB, 6 * SUB):
-        pass_z(at)
+    emb_final[...] = emb_full[...].reshape(vocab_rows, LANES)[:vocab, :width]
+    stores = [
+        pltpu.make_async_copy(src, dst, out_sem.at[2 * SUB + k])
+        for k, (src, dst) in enumerate(
+            (
+                (iw_final, out_iw),
+                (gb_final, out_gb),
+                (loss_final, out_loss),
+                (decb_final, out_decb),
+                (dec_final, out_dec),
+                (emb_final, out_emb),
+            )
+        )
+    ]
+    for each in stores[2:]:
+        each.start()
     spot = giw_full.at[1 - z_low]
     copy(spot, spot, giw_sem, (4,), (2, 0)).wait_recv()
     for side in range(2):
@@ -783,16 +923,19 @@
             for run in range(runs):
                 to = slice((run * 2 + side) * LANES, (run * 2 + side + 1) * LANES)
                 lanes = slice(run * LANES, (run + 1) * LANES)
-                out_iw[gate, :, to] = value[:width, lanes]
-                out_gb[gate : gate + 1, to] = value[width : width + 1, lanes]
-    for at in range(6 * SUB, 8 * SUB):
+                iw_final[:, gate, to] = value[:width, lanes]
+                gb_final[gate : gate + 1, to] = value[width : width + 1, lanes]
+    for each in stores[:2]:
+        each.start()
+    for at in range(12, 16):
         pass_z(at)
 
     def scatter(here, side, gate, value):
         for run in range(runs):
-            at = pl.multiple_of(gate * 2 * units + run * 2 * LANES + side * LANES, LANES)
-            out_rec[here, pl.ds(at, LANES)] = value[:, run * LANES : (run + 1) * LANES]
-
+            at = pl.multiple_of((run * 2 + side) * LANES, LANES)
+            rec_final[here, gate, pl.ds(at, LANES)] = value[:, run * LANES : (run + 1) * LANES]
+
+    rec_stores = []
     for side in range(2):
         for sub in range(SUB):
             z_copy(0, side, sub).wait_recv()
@@ -814,46 +957,28 @@
                     gate,
                     z_in[1, side, mine, lanes].astype(f32) + z_in[2, side, mine, lanes].astype(f32),
                 )
-
-    ids_copy.wait_send()
-    dec_z.wait_send()
-    for each in dec_x + dec_sends + dec_relays + iw_copies + [small_copy]:
-        each.wait_send()
-    for p in range(PIECES):
-        for at in range(8):
-            weight_core(block_of(at), at, p).wait_send()
-        for k in range(3):
-            weight_z(k, p).wait_send()
-        for k in range(4):
-            weight_x(k, p).wait_send()
-
-    def sent(t, _):
-        for s in range(SPLIT):
-            for j in range(3):
-                hidden_copy(t, s, j).wait_send()
-            hidden_core(t, s).wait_send()
-            lg_copy(t, s).wait_send()
-            pg_copy(t, s).wait_send()
-        return 0
-
-    lax.fori_loop(0, steps, sent, 0)
-
-    def sent_back(t, _):
-        for s in range(SPLIT):
-            pgm_copy(t, s).wait_send()
-            for j in range(3):
-                chip_copy(t, s, j).wait_send()
-        return 0
-
-    lax.fori_loop(1, steps, sent_back, 0)
-    for at, spot in enumerate(order):
-        x_copy(*spot).wait_send()
-        if spot[0] < 3 and at not in range(4 * SUB - 2):
-            z_copy(*spot).wait_send()
-    for each in [giw_x, giw_z, giw_back_z, giw_back_x, giw_side, dsum_x, dsum_z]:
+            rec_stores.append(
+                pltpu.make_async_copy(
+                    rec_final.at[here], out_rec.at[here], out_sem.at[side * SUB + sub]
+                )
+            )
+            rec_stores[-1].start()
+
+    for each in rec_stores + stores:
+        each.wait()
+    for each in [giw_x, giw_z, giw_back_z, giw_back_x, giw_side]:
         each.wait_send()
     for each in emb_copies + emb2 + emb3:
         each.wait_send()
+    for at, spot in enumerate(order):
+        x_copy(*spot).wait_send()
+        if spot[0] < 3 and at not in range(3 * SUB):
+            z_copy(*spot).wait_send()
+
+
+def hand_over(*refs):
+    for src, dst in zip(refs[:7], refs[7:]):
+        dst[...] = src[...].reshape(dst.shape)
 
 
 def grouped(
@@ -889,6 +1014,7 @@
     dec = decoder_weight.reshape(dec_rows, vocab)
 
     vmem = pl.BlockSpec(memory_space=pltpu.VMEM)
+    anywhere = pl.BlockSpec(memory_space=pl.ANY)
     dims = (steps, rows, units, vocab, vocab_pad, tokens_all, block)
 
     def sems(*shape):
@@ -899,19 +1025,28 @@
         out_shape=[
             jax.ShapeDtypeStruct((1, 1), f32),
             jax.ShapeDtypeStruct((vocab, width), f32),
-            jax.ShapeDtypeStruct((4, width, local_units), f32),
-            jax.ShapeDtypeStruct((block, 2 * cols), f32),
+            jax.ShapeDtypeStruct((width, 4, local_units), f32),
+            jax.ShapeDtypeStruct((block, 4, local_units), f32),
             jax.ShapeDtypeStruct((4, local_units), f32),
             jax.ShapeDtypeStruct((dec_rows, vocab), f32),
             jax.ShapeDtypeStruct((1, vocab), f32),
         ],
-        in_specs=[vmem] * 9,
-        out_specs=[vmem] * 7,
+        in_specs=[vmem] * 4 + [anywhere] * 2 + [vmem] * 3,
+        out_specs=[anywhere] * 7,
         scratch_shapes=[
+            pltpu.VMEM((block, 4, local_units), bf16),
+            pltpu.VMEM((width, 4, local_units), bf16),
+            pltpu.VMEM((block, 4, local_units), f32),
+            pltpu.VMEM((width, 4, local_units), f32),
+            pltpu.VMEM((4, local_units), f32),
+            pltpu.VMEM((1, 1), f32),
+            pltpu.VMEM((1, vocab), f32),
+            pltpu.VMEM((dec_rows, vocab), f32),
+            pltpu.VMEM((vocab, width), f32),
             pltpu.VMEM((2, LANES, row_count), jnp.int32),
             pltpu.VMEM((row_count, LANES), jnp.int32),
-            pltpu.VMEM((2, block, cols), bf16),
-            pltpu.VMEM((2, 8, units, cols), bf16),
+            pltpu.VMEM((2, 4, block, units), bf16),
+            pltpu.VMEM((2, 8, 4, units, units), bf16),
             pltpu.VMEM((vocab_rows, LANES), bf16),
             pltpu.VMEM((2, LANES, cols), bf16),
             pltpu.VMEM((2, 1, cols), f32),
@@ -959,10 +1094,12 @@
             pltpu.VMEM((2, dec_rows, vocab_pad), bf16),
             pltpu.VMEM((dec_rows, vocab_pad), bf16),
             pltpu.VMEM((dec_rows, vocab_pad), bf16),
+            pltpu.SemaphoreType.DMA((PIECES + 2,)),
+            pltpu.SemaphoreType.DMA((2 * SUB + 6,)),
             sems(1),
-            sems(3, PIECES),
-            sems(4, PIECES),
-            sems(8, PIECES),
+            sems(3, PIECES + 1),
+            sems(4, PIECES + 1),
+            sems(8, PIECES + 1),
             sems(2),
             sems(3),
             sems(7),
@@ -989,20 +1126,36 @@
         next_chars.T,
         resets.T,
         embedding,
-        in_by_gate,
-        by_gate,
+        input_weight,
+        recurrent_weight,
         gate_bias,
         dec,
-        decoder_bias.reshape(1, vocab),
-    )
+        decoder_bias,
+    )
+    results = [loss, emb_grad, in_grad, rec_grad, bias_grad, dec_grad, dec_bias_grad]
+    parts = 2
+    blocks = [
+        pl.BlockSpec((each.shape[0] // parts,) + each.shape[1:], lambda i: (i, 0, 0))
+        if each.ndim == 3
+        else pl.BlockSpec(each.shape, lambda i: (0, 0))
+        for each in results
+    ]
+    loss, emb_grad, in_grad, rec_grad, bias_grad, dec_grad, dec_bias_grad = pl.pallas_call(
+        hand_over,
+        out_shape=[jax.ShapeDtypeStruct(each.shape, f32) for each in results[:-1]]
+        + [jax.ShapeDtypeStruct((vocab,), f32)],
+        grid=(parts,),
+        in_specs=blocks,
+        out_specs=blocks[:-1] + [pl.BlockSpec((vocab,), lambda i: (0,))],
+    )(*results)
     return (
         loss.reshape(()),
         emb_grad,
-        in_grad.transpose(1, 0, 2),
-        rec_grad.reshape(recurrent_weight.shape),
+        in_grad,
+        rec_grad,
         bias_grad,
         dec_grad.reshape(decoder_weight.shape),
-        dec_bias_grad.reshape(vocab),
+        dec_bias_grad,
     )
 
 

time: 230 us -> 206 us (0.90)
  local copies, waits for them, and re-layouts: 13 us -> 0 us
  Pallas kernels: 214 us -> 203 us
    pallas_call x1, Pallas kernels: 214 us -> 199 us  [grouped(): pl.pallas_call(functools.partial(layer_kernel, dims), out_shape=[jax.Shap...]
    unnamed x16 -> x0, local copies, waits for them, and re-layouts: 8.72 us -> none
    reshape x2 -> x0, local copies, waits for them, and re-layouts: 4.23 us -> none  [the longest x1 3.67 us: grouped(): rec_grad.reshape(recurrent_weight.shape)]
    pallas_call x0 -> x1, Pallas kernels: none -> 3.87 us  [grouped(): pl.pallas_call(hand_over, out_shape=[jax.ShapeDtypeStruct(each.shape, f32...]
where the time goes in v3:
time: 206 us; the launch traced here: 204 us
  Pallas kernels  203 us (99%)
    pallas_call x1, Pallas kernels, grouped(): pl.pallas_call(functools.partial(layer_kernel, dims), out_shape=[jax.Shap...  199 us

profile of v3, /device:TPU:1, one launch (start us, length us, event | category | flops | bytes accessed | tf_op | source)
XLA Modules:
  0.0 203.8 jit_solution(5349991575667839313)
XLA Ops:
  0.6 199.1 %shard_map.144 = (f32[1,1]{1,0:T(1,128)}, f32[275,100]{1,0:T(8,128)}, f32[100,4,512]{2,1,0:T(4,128)}, f32[256,4,512]{2,1,0:T(4,128)}, f32[4,512]{1,0:T(4,128)}, /*index=5*/f32[64,275]{1,0:T(8,128)}, f32[1,275]{1,0:T(1,128)}) custom-call(s32[6,128]{1,0:T(8,128)} %bitcast.7, s32[6,128]{1,0:T(8,128)} %bitcast.8, s32[6,128]{1,0:T(8,128)} %bitcast.9, ...), custom_call_target="tpu_custom_call" | custom-call | tf_op jit(solution)/shard_map/pallas_call | solution.py:1023
  199.7 3.9 %shard_map.145 = (f32[1,1]{1,0:T(1,128)}, f32[275,100]{1,0:T(8,128)}, f32[100,4,512]{2,1,0:T(4,128)}, f32[256,4,512]{2,1,0:T(4,128)}, f32[4,512]{1,0:T(4,128)}, /*index=5*/f32[64,275]{1,0:T(8,128)}, f32[275]{0:T(512)}) custom-call(f32[1,1]{1,0:T(1,128)} %get-tuple-element.21.refs_0_, f32[275,100]{1,0:T(8,128)} %get-tuple-element.22.refs_1_, ...), custom_call_target="tpu_custom_call" | custom-call | tf_op jit(solution)/shard_map/pallas_call | solution.py:1143

commit v4 on v3

--- a/solution.py
+++ b/solution.py
@@ -82,6 +82,8 @@
     hid,
     gates,
     cells,
+    squashes,
+    from_logits,
     onehots,
     embedded,
     keeps,
@@ -100,7 +102,6 @@
     small_acc,
     small_pair,
     both,
-    acc,
     x_out,
     x_in,
     z_out,
@@ -392,7 +393,9 @@
             if added is not None:
                 cell = forget * keep * cells[t - 1, c, here] + cell
             cells[t, c, here] = cell
-            hid[z_low * 4 + y_at * 2 + c, t, wide(s)] = (out_gate * jnp.tanh(cell)).astype(bf16)
+            squash = jnp.tanh(cell)
+            hid[z_low * 4 + y_at * 2 + c, t, wide(s)] = (out_gate * squash).astype(bf16)
+            squashes[t, c, here] = squash
             gates[t, c, here, :units] = in_gate
             gates[t, c, here, units : 2 * units] = forget
             gates[t, c, here, 2 * units : 3 * units] = candidate
@@ -400,8 +403,8 @@
         for j in (2, 0, 1):
             hidden_copy(t, s, j).start()
 
-    def add_slot(total, t, s, at):
-        some = hid[at, t, wide(s)]
+    def add_slot(total, t, here, at):
+        some = hid[at, t, here]
         for c in range(2):
             for gate in range(4):
                 more = dot(some, weights[c, at, gate])
@@ -440,30 +443,41 @@
     for s in range(SPLIT):
         for j in range(3):
             hidden_in(0, s, j).wait_recv()
-        total = [[None] * 4, [None] * 4]
-        for at in range(4):
-            add_slot(total, 0, s, at)
-        for c in range(2):
-            for gate in range(4):
-                lanes = slice(gate * units, (gate + 1) * units)
-                gates[1, c, span(s), lanes] += keeps[1, span(s), :1] * total[c][gate]
+    mine = pl.ds(pl.multiple_of(core * half, half), half)
+    total = [[None] * 4, [None] * 4]
+    for at in range(4):
+        add_slot(total, 0, mine, at)
+    for c in range(2):
+        for gate in range(4):
+            lanes = slice(gate * units, (gate + 1) * units)
+            gates[1, c, :, lanes] += keeps[1, :, :1] * total[c][gate]
     for p in range(6, PIECES + 1):
         weight_round(p)
     for p in range(PIECES + 1 - LAG, PIECES + 1):
         weight_over_x(p)
     weights_from_core(range(PIECES // 2, PIECES + 1))
 
-    dec_relays = []
-    for j in range(3):
+    def dec_relay(j):
         spot = dec_all.at[slot(CHIPS[j])]
-        copy(spot, spot, decr_sem, (j,), CHIPS[j]).wait_recv()
-        dec_relays.append(copy(spot, spot, decr_sem, (4 + j,), (0, 1)))
-        dec_relays[-1].start()
+        return copy(spot, spot, decr_sem, (4 + j,), (0, 1))
+
+    def pass_decoder():
+        for j in range(3):
+            spot = dec_all.at[slot(CHIPS[j])]
+            copy(spot, spot, decr_sem, (j,), CHIPS[j]).wait_recv()
+            dec_relay(j).start()
+
+    def weight_sent():
+        for p in range(PIECES + 1):
+            for at in range(8):
+                weight_core(block_of(at), at, p).wait_send()
+            for k in range(4):
+                weight_x(k, p).wait_send()
 
     def add_chip(total, t, s, flips):
         first = turn(z_low, flips[0] // 2) * 4 + turn(y_at, flips[1] // 2) * 2
         for k in range(2):
-            add_slot(total, t, s, first + k)
+            add_slot(total, t, wide(s), first + k)
 
     def gather_hidden(t, s):
         total = [[None] * 4, [None] * 4]
@@ -496,6 +510,8 @@
         grad = ((exps / total - jnp.where(hot, 1.0, 0.0)) / tokens_all).astype(bf16)
         logit_grads[t, wide(s)] = grad
         lg_copy(t, s).start()
+        for c in range(2):
+            from_logits[t, c, here] = dot_t(grad, dec_all[z_low * 4 + y_at * 2 + c])
         small_acc[...] += jnp.sum(grad.astype(f32), axis=0, keepdims=True) + jnp.where(
             last_lane, jnp.sum(lost, axis=0, keepdims=True) / tokens_all, 0.0
         )
@@ -506,12 +522,22 @@
             decode(t - 1, s)
         return 0
 
+    @pl.when(core == 1)
+    def _():
+        pass_decoder()
+
+    total = [[None] * 4, [None] * 4]
+    for at in range(4, 8):
+        add_slot(total, 0, mine, at)
     for s in range(SPLIT):
-        total = [[None] * 4, [None] * 4]
-        for at in range(4, 8):
-            add_slot(total, 0, s, at)
-        cell_step(1, s, total)
+        here = slice(s * part, (s + 1) * part)
+        cell_step(1, s, [[more[here] for more in total[c]] for c in range(2)])
         hidden_core(0, s).start()
+
+    @pl.when(core == 0)
+    def _():
+        pass_decoder()
+
     spot = dec_all.at[slot((0, 1))]
     copy(spot, spot, decr_sem, (3,), (0, 1)).wait_recv()
     for j in range(3):
@@ -534,14 +560,14 @@
         if not first:
             keep = keeps[t, here, :1]
         for c in range(2):
-            hidden_grad = dot_t(logit_grads[t, wide(s)], dec_all[z_low * 4 + y_at * 2 + c])
+            hidden_grad = from_logits[t, c, here]
             if carried is not None:
                 hidden_grad = hidden_grad + carried[:, c * units : (c + 1) * units]
             in_gate = gates[t, c, here, :units]
             forget = gates[t, c, here, units : 2 * units]
             candidate = gates[t, c, here, 2 * units : 3 * units]
             out_gate = gates[t, c, here, 3 * units :]
-            squash = jnp.tanh(cells[t, c, here])
+            squash = squashes[t, c, here]
             cell_grad = hidden_grad * out_gate * (1.0 - squash * squash)
             if carried is not None:
                 cell_grad = cell_grad + carry_c[c, here]
@@ -605,11 +631,7 @@
 
     last = steps - 1
 
-    for p in range(PIECES + 1):
-        for at in range(8):
-            weight_core(block_of(at), at, p).wait_send()
-        for k in range(4):
-            weight_x(k, p).wait_send()
+    weight_sent()
 
     def turn_over(at, _):
         for c in range(2):
@@ -679,7 +701,12 @@
 
         return 0
 
-    lax.fori_loop(1, last, backward, 0)
+    lax.fori_loop(1, last - 1, backward, 0)
+    for s in range(SPLIT):
+        cell_back(1, s, carried_in(1, s), False)
+        share(1, s, False)
+
+    acc = gates.at[pl.ds(steps - 4, 4)]
 
     far = (2, 3, 1, 0)
 
@@ -716,6 +743,20 @@
         ).reshape(2, LANES, cols)
         x_out[k, side] = both[1 - x_at].astype(bf16)
         acc[k, side] = both[x_at]
+
+    def weight_grad_first(side):
+        at = side * 4 + turn(z_at, far[0])
+        for k in (1, 0):
+            lanes = pl.ds(pl.multiple_of((x_at if k == 0 else 1 - x_at) * LANES, LANES), LANES)
+            some = t_dot(
+                hid[at, 0 : steps - 1, :, lanes].reshape(used, LANES),
+                pgm[...].reshape(used, cols),
+            )
+            if k:
+                x_out[0, side] = some.astype(bf16)
+                send_eighth(2 * side, 2 * side + 1)
+            else:
+                acc[0, side] = some
 
     order = [(k, side, sub) for k in range(4) for side in range(2) for sub in range(SUB)]
 
@@ -737,15 +778,49 @@
             acc[k, side, here] = total
             return
         z_out[k, side, here] = total.astype(bf16)
-        if at in range(SUB, 4 * SUB):
-            z_copy(*order[at - SUB]).wait_send()
+        if at in range(3, 4 * SUB):
+            z_copy(*order[at - 3]).wait_send()
         z_copy(k, side, sub).start()
 
-    weight_grad(0, 0)
-    send_eighth(0, 1)
+    rec_stores = []
+
+    def scatter(here, side, gate, value):
+        for run in range(runs):
+            at = pl.multiple_of((run * 2 + side) * LANES, LANES)
+            rec_final[here, gate, pl.ds(at, LANES)] = value[:, run * LANES : (run + 1) * LANES]
+
+    def finish(at):
+        pass_z(12 + at)
+        for which in range(at * (SUB // 2), (at + 1) * (SUB // 2)):
+            side, sub = divmod(which, SUB)
+            for k in range(3):
+                z_copy(k, side, sub).wait_recv()
+            here = pl.ds(side * LANES + sub * piece_rows, piece_rows)
+            mine = pl.ds(sub * piece_rows, piece_rows)
+            for gate in range(4):
+                lanes = slice(gate * units, (gate + 1) * units)
+                value = acc[3, side, mine, lanes] + z_in[0, side, mine, lanes].astype(f32)
+                scatter(here, z_low, gate, value)
+                value = z_in[1, side, mine, lanes].astype(f32) + z_in[2, side, mine, lanes].astype(
+                    f32
+                )
+                scatter(here, 1 - z_low, gate, value)
+            rec_stores.append(
+                pltpu.make_async_copy(rec_final.at[here], out_rec.at[here], out_sem.at[which])
+            )
+            rec_stores[-1].start()
+
+    weight_grad_first(0)
     weight_grad(0, 1)
     send_eighth(2, 3)
-    pass_z(0)
+    for s in range(SPLIT):
+        spread(1, s)
+    pass_piece(0)
+    pass_piece(1)
+    weight_grad(1, 0)
+    pass_piece(2)
+    weight_grad(2, 0)
+    pass_piece(3)
 
     for s in range(SPLIT):
         cell_back(0, s, carried_in(0, s), True)
@@ -763,10 +838,8 @@
         giw_out[k] = giw_acc[:, pl.ds(at, units)].astype(bf16)
     giw_x = copy(giw_out, giw_x_in, giw_sem, (0,), (1, 0))
     giw_x.start()
-    pass_z(1)
-    weight_grad(1, 0)
-    weight_grad(2, 0)
     send_eighth(4, 8)
+    pass_piece(4)
 
     emb_rows = emb_full.shape[1]
     by_char = jnp.zeros((vocab_rows, 2 * LANES), f32)
@@ -783,10 +856,8 @@
     for each in emb_copies:
         each.start()
     emb_in[own] = emb_part[own]
-    pass_z(2)
+    pass_piece(5)
     weight_grad(1, 1)
-    weight_grad(2, 1)
-    send_eighth(5, 9)
 
     giw_x.wait_recv()
     for k in range(2):
@@ -797,6 +868,8 @@
     ].astype(bf16)
     giw_z = copy(giw_z_out, giw_z_in, giw_sem, (1,), (4, 0))
     giw_z.start()
+    send_eighth(5, 9)
+    pass_piece(6)
     for j, flips in enumerate(GROUP):
         spot = emb_in.at[slot(flips)]
         copy(spot, spot, emb_sem, (j,), flips).wait_recv()
@@ -819,12 +892,11 @@
     emb2 = [copy(spot, spot, emb2_sem, (j,), (flips, 0)) for j, flips in enumerate(OTHERS)]
     for each in emb2:
         each.start()
-    pass_z(3)
+    weight_grad(2, 1)
+    pass_piece(7)
+    send_eighth(6, 10)
     weight_grad(3, 0)
     weight_grad(3, 1)
-    pass_z(4)
-    pass_z(8)
-    send_eighth(6, 10)
 
     giw_z.wait_recv()
     gate_at = x_at * 2 + z_high
@@ -834,9 +906,18 @@
     spot = giw_full.at[z_low, gate_at]
     giw_back_z = copy(spot, spot, giw_sem, (2,), (4, 0))
     giw_back_z.start()
-    pass_z(5)
-    pass_z(9)
-    send_eighth(7, 11, 12, 13)
+
+    giw_turn = (gate_at, x_at * 2 + 1 - z_high, (1 - x_at) * 2, (1 - x_at) * 2 + 1)
+
+    def giw_side(k, half_at):
+        spot = giw_full.at[half_at, giw_turn[k]]
+        return copy(spot, spot, giw_sem, (4 + k,), (2, 0))
+
+    giw_side(0, z_low).start()
+    pass_piece(8)
+    send_eighth(7, 11)
+    pass_piece(9)
+    pass_z(8)
     for j, flips in enumerate(OTHERS):
         spot = emb_sums.at[place(flips)]
         copy(spot, spot, emb2_sem, (j,), (flips, 0)).wait_recv()
@@ -853,49 +934,24 @@
     loss_final[...] = sums[emb_rows + k : emb_rows + k + 1, LANES - 1 :]
     spot = giw_full.at[z_low, x_at * 2 + 1 - z_high]
     copy(spot, spot, giw_sem, (2,), (4, 0)).wait_recv()
+    giw_side(1, z_low).start()
     spot = giw_full.at[z_low, pl.ds(x_at * 2, 2)]
     giw_back_x = copy(spot, spot, giw_sem, (3,), (1, 0))
     giw_back_x.start()
-    send_eighth(14, 15)
-    pass_z(6)
+    send_eighth(12, 13, 14, 15)
+    pass_piece(10)
+    pass_z(9)
+    pass_piece(11)
+    spot = giw_full.at[z_low, pl.ds((1 - x_at) * 2, 2)]
+    copy(spot, spot, giw_sem, (3,), (1, 0)).wait_recv()
+    giw_side(2, z_low).start()
+    pass_piece(12)
     pass_z(10)
     dsum_z(1).wait_recv()
     total = dec_part[z_high, x_at] + dec_x_in[z_high].astype(f32) + dec_z_in[...].astype(f32)
     dec_final[...] = total[:, :vocab]
-    spot = giw_full.at[z_low, pl.ds((1 - x_at) * 2, 2)]
-    copy(spot, spot, giw_sem, (3,), (1, 0)).wait_recv()
-    spot = giw_full.at[z_low]
-    giw_side = copy(spot, spot, giw_sem, (4,), (2, 0))
-    giw_side.start()
-    pass_z(7)
+    pass_piece(13)
     pass_z(11)
-    ids_copy.wait_send()
-    dec_z.wait_send()
-    for each in dec_x + dec_sends + dec_relays + iw_copies + [small_copy(), dsum_x(), dsum_z(1)]:
-        each.wait_send()
-    for p in range(PIECES + 1):
-        for k in range(3):
-            weight_z(k, p).wait_send()
-
-    def sent(t, _):
-        for s in range(SPLIT):
-            for j in range(3):
-                hidden_copy(t, s, j).wait_send()
-            hidden_core(t, s).wait_send()
-            lg_copy(t, s).wait_send()
-            pg_copy(t, s).wait_send()
-        return 0
-
-    lax.fori_loop(0, steps, sent, 0)
-
-    def sent_back(t, _):
-        for s in range(SPLIT):
-            pgm_copy(t, s).wait_send()
-            for j in range(3):
-                chip_copy(t, s, j).wait_send()
-        return 0
-
-    lax.fori_loop(1, steps, sent_back, 0)
     for j, flips in enumerate(GROUP):
         spot = emb_full.at[slot(flips)]
         copy(spot, spot, emb3_sem, (j,), flips).wait_recv()
@@ -915,8 +971,42 @@
     ]
     for each in stores[2:]:
         each.start()
-    spot = giw_full.at[1 - z_low]
-    copy(spot, spot, giw_sem, (4,), (2, 0)).wait_recv()
+    finish(0)
+    giw_side(3, z_low).start()
+    pass_piece(14)
+    ids_copy.wait_send()
+    dec_z.wait_send()
+    for each in dec_x + dec_sends + [dec_relay(j) for j in range(3)] + iw_copies + [small_copy(), dsum_x(), dsum_z(1)]:
+        each.wait_send()
+    for p in range(PIECES + 1):
+        for k in range(3):
+            weight_z(k, p).wait_send()
+
+    def sent(t, _):
+        for s in range(SPLIT):
+            for j in range(3):
+                hidden_copy(t, s, j).wait_send()
+            hidden_core(t, s).wait_send()
+            lg_copy(t, s).wait_send()
+            pg_copy(t, s).wait_send()
+        return 0
+
+    lax.fori_loop(0, steps, sent, 0)
+
+    def sent_back(t, _):
+        for s in range(SPLIT):
+            pgm_copy(t, s).wait_send()
+            for j in range(3):
+                chip_copy(t, s, j).wait_send()
+        return 0
+
+    lax.fori_loop(1, steps, sent_back, 0)
+    finish(1)
+    pass_piece(15)
+    finish(2)
+    finish(3)
+    for k in range(4):
+        giw_side(k, 1 - z_low).wait_recv()
     for side in range(2):
         for gate in range(4):
             value = giw_full[side, gate].astype(f32)
@@ -927,52 +1017,18 @@
                 gb_final[gate : gate + 1, to] = value[width : width + 1, lanes]
     for each in stores[:2]:
         each.start()
-    for at in range(12, 16):
-        pass_z(at)
-
-    def scatter(here, side, gate, value):
-        for run in range(runs):
-            at = pl.multiple_of((run * 2 + side) * LANES, LANES)
-            rec_final[here, gate, pl.ds(at, LANES)] = value[:, run * LANES : (run + 1) * LANES]
-
-    rec_stores = []
-    for side in range(2):
-        for sub in range(SUB):
-            z_copy(0, side, sub).wait_recv()
-            z_copy(1, side, sub).wait_recv()
-            z_copy(2, side, sub).wait_recv()
-            here = pl.ds(side * LANES + sub * piece_rows, piece_rows)
-            mine = pl.ds(sub * piece_rows, piece_rows)
-            for gate in range(4):
-                lanes = slice(gate * units, (gate + 1) * units)
-                scatter(
-                    here,
-                    z_low,
-                    gate,
-                    acc[3, side, mine, lanes] + z_in[0, side, mine, lanes].astype(f32),
-                )
-                scatter(
-                    here,
-                    1 - z_low,
-                    gate,
-                    z_in[1, side, mine, lanes].astype(f32) + z_in[2, side, mine, lanes].astype(f32),
-                )
-            rec_stores.append(
-                pltpu.make_async_copy(
-                    rec_final.at[here], out_rec.at[here], out_sem.at[side * SUB + sub]
-                )
-            )
-            rec_stores[-1].start()
 
     for each in rec_stores + stores:
         each.wait()
-    for each in [giw_x, giw_z, giw_back_z, giw_back_x, giw_side]:
+    for each in [giw_x, giw_z, giw_back_z, giw_back_x]:
         each.wait_send()
+    for k in range(4):
+        giw_side(k, z_low).wait_send()
     for each in emb_copies + emb2 + emb3:
         each.wait_send()
     for at, spot in enumerate(order):
         x_copy(*spot).wait_send()
-        if spot[0] < 3 and at not in range(3 * SUB):
+        if spot[0] < 3 and at not in range(4 * SUB - 3):
             z_copy(*spot).wait_send()
 
 
@@ -1056,6 +1112,8 @@
             pltpu.VMEM((8, steps, rows, units), bf16),
             pltpu.VMEM((steps, 2, half, cols), f32),
             pltpu.VMEM((steps, 2, half, units), f32),
+            pltpu.VMEM((steps, 2, half, units), f32),
+            pltpu.VMEM((steps, 2, half, units), f32),
             pltpu.VMEM((steps, vocab_rows, rows), bf16),
             pltpu.VMEM((steps, rows, LANES), bf16),
             pltpu.VMEM((steps, half, LANES), f32),
@@ -1074,7 +1132,6 @@
             pltpu.VMEM((1, vocab_pad), f32),
             pltpu.VMEM((2, 1, vocab_pad), f32),
             pltpu.VMEM((2, LANES, cols), f32),
-            pltpu.VMEM((4, 2, LANES, cols), f32),
             pltpu.VMEM((4, 2, LANES, cols), bf16),
             pltpu.VMEM((4, 2, LANES, cols), bf16),
             pltpu.VMEM((3, 2, LANES, cols), bf16),
@@ -1112,7 +1169,7 @@
             sems(steps - 1, SPLIT, 3),
             sems(4, 2, SUB),
             sems(3, 2, SUB),
-            sems(5),
+            sems(8),
             sems(7),
             sems(3),
             sems(7),

time: 206 us -> 201 us (0.976)
  Pallas kernels: 203 us -> 200 us
    pallas_call x1, Pallas kernels: 199 us -> 196 us  [grouped(): pl.pallas_call(functools.partial(layer_kernel, dims), out_shape=[jax.Shap...]
where the time goes in v4:
time: 201 us
  Pallas kernels  200 us (100%)
    pallas_call x1, Pallas kernels, grouped(): pl.pallas_call(functools.partial(layer_kernel, dims), out_shape=[jax.Shap...  196 us

profile of v4, /device:TPU:1, one launch (start us, length us, event | category | flops | bytes accessed | tf_op | source)
XLA Modules:
  0.0 200.7 jit_solution(1346883478329979036)
XLA Ops:
  0.6 196.0 %shard_map.144 = (f32[1,1]{1,0:T(1,128)}, f32[275,100]{1,0:T(8,128)}, f32[100,4,512]{2,1,0:T(4,128)}, f32[256,4,512]{2,1,0:T(4,128)}, f32[4,512]{1,0:T(4,128)}, /*index=5*/f32[64,275]{1,0:T(8,128)}, f32[1,275]{1,0:T(1,128)}) custom-call(s32[6,128]{1,0:T(8,128)} %bitcast.7, s32[6,128]{1,0:T(8,128)} %bitcast.8, s32[6,128]{1,0:T(8,128)} %bitcast.9, ...), custom_call_target="tpu_custom_call" | custom-call | tf_op jit(solution)/shard_map/pallas_call | solution.py:1079
  196.7 3.9 %shard_map.145 = (f32[1,1]{1,0:T(1,128)}, f32[275,100]{1,0:T(8,128)}, f32[100,4,512]{2,1,0:T(4,128)}, f32[256,4,512]{2,1,0:T(4,128)}, f32[4,512]{1,0:T(4,128)}, /*index=5*/f32[64,275]{1,0:T(8,128)}, f32[275]{0:T(512)}) custom-call(f32[1,1]{1,0:T(1,128)} %get-tuple-element.21.refs_0_, f32[275,100]{1,0:T(8,128)} %get-tuple-element.22.refs_1_, ...), custom_call_target="tpu_custom_call" | custom-call | tf_op jit(solution)/shard_map/pallas_call | solution.py:1200

commit v5 on v4

--- a/solution.py
+++ b/solution.py
@@ -62,13 +62,6 @@
     out_decb,
     rec_in,
     iw_in,
-    rec_final,
-    iw_final,
-    gb_final,
-    loss_final,
-    decb_final,
-    dec_final,
-    emb_final,
     ids_rows,
     ids_cols,
     rec_halves,
@@ -122,7 +115,6 @@
     dec_z_out,
     dec_z_in,
     in_sem,
-    out_sem,
     ids_sem,
     wz_sem,
     wx_sem,
@@ -782,12 +774,10 @@
             z_copy(*order[at - 3]).wait_send()
         z_copy(k, side, sub).start()
 
-    rec_stores = []
-
     def scatter(here, side, gate, value):
         for run in range(runs):
             at = pl.multiple_of((run * 2 + side) * LANES, LANES)
-            rec_final[here, gate, pl.ds(at, LANES)] = value[:, run * LANES : (run + 1) * LANES]
+            out_rec[here, gate, pl.ds(at, LANES)] = value[:, run * LANES : (run + 1) * LANES]
 
     def finish(at):
         pass_z(12 + at)
@@ -805,10 +795,6 @@
                     f32
                 )
                 scatter(here, 1 - z_low, gate, value)
-            rec_stores.append(
-                pltpu.make_async_copy(rec_final.at[here], out_rec.at[here], out_sem.at[which])
-            )
-            rec_stores[-1].start()
 
     weight_grad_first(0)
     weight_grad(0, 1)
@@ -929,9 +915,9 @@
         each.start()
     for k in range(vocab_pad // LANES):
         lanes = slice(k * LANES, min(vocab, (k + 1) * LANES))
-        decb_final[:, lanes] = sums[emb_rows + k : emb_rows + k + 1, : lanes.stop - lanes.start]
+        out_decb[:, lanes] = sums[emb_rows + k : emb_rows + k + 1, : lanes.stop - lanes.start]
     k = vocab_pad // LANES - 1
-    loss_final[...] = sums[emb_rows + k : emb_rows + k + 1, LANES - 1 :]
+    out_loss[...] = sums[emb_rows + k : emb_rows + k + 1, LANES - 1 :]
     spot = giw_full.at[z_low, x_at * 2 + 1 - z_high]
     copy(spot, spot, giw_sem, (2,), (4, 0)).wait_recv()
     giw_side(1, z_low).start()
@@ -949,28 +935,13 @@
     pass_z(10)
     dsum_z(1).wait_recv()
     total = dec_part[z_high, x_at] + dec_x_in[z_high].astype(f32) + dec_z_in[...].astype(f32)
-    dec_final[...] = total[:, :vocab]
+    out_dec[...] = total[:, :vocab]
     pass_piece(13)
     pass_z(11)
     for j, flips in enumerate(GROUP):
         spot = emb_full.at[slot(flips)]
         copy(spot, spot, emb3_sem, (j,), flips).wait_recv()
-    emb_final[...] = emb_full[...].reshape(vocab_rows, LANES)[:vocab, :width]
-    stores = [
-        pltpu.make_async_copy(src, dst, out_sem.at[2 * SUB + k])
-        for k, (src, dst) in enumerate(
-            (
-                (iw_final, out_iw),
-                (gb_final, out_gb),
-                (loss_final, out_loss),
-                (decb_final, out_decb),
-                (dec_final, out_dec),
-                (emb_final, out_emb),
-            )
-        )
-    ]
-    for each in stores[2:]:
-        each.start()
+    out_emb[...] = emb_full[...].reshape(vocab_rows, LANES)[:vocab, :width]
     finish(0)
     giw_side(3, z_low).start()
     pass_piece(14)
@@ -1013,13 +984,9 @@
             for run in range(runs):
                 to = slice((run * 2 + side) * LANES, (run * 2 + side + 1) * LANES)
                 lanes = slice(run * LANES, (run + 1) * LANES)
-                iw_final[:, gate, to] = value[:width, lanes]
-                gb_final[gate : gate + 1, to] = value[width : width + 1, lanes]
-    for each in stores[:2]:
-        each.start()
-
-    for each in rec_stores + stores:
-        each.wait()
+                out_iw[:, gate, to] = value[:width, lanes]
+                out_gb[gate : gate + 1, to] = value[width : width + 1, lanes]
+
     for each in [giw_x, giw_z, giw_back_z, giw_back_x]:
         each.wait_send()
     for k in range(4):
@@ -1033,8 +1000,17 @@
 
 
 def hand_over(*refs):
-    for src, dst in zip(refs[:7], refs[7:]):
-        dst[...] = src[...].reshape(dst.shape)
+    sources, places, flat, sems = list(refs[:7]), refs[7:14], refs[14], refs[15]
+    flat[...] = sources[6][...].reshape(flat.shape)
+    sources[6] = flat
+    copies = [
+        pltpu.make_async_copy(src, dst, sems.at[k])
+        for k, (src, dst) in enumerate(zip(sources, places))
+    ]
+    for each in copies:
+        each.start()
+    for each in copies:
+        each.wait()
 
 
 def grouped(
@@ -1079,26 +1055,19 @@
     loss, emb_grad, in_grad, rec_grad, bias_grad, dec_grad, dec_bias_grad = pl.pallas_call(
         functools.partial(layer_kernel, dims),
         out_shape=[
-            jax.ShapeDtypeStruct((1, 1), f32),
-            jax.ShapeDtypeStruct((vocab, width), f32),
-            jax.ShapeDtypeStruct((width, 4, local_units), f32),
-            jax.ShapeDtypeStruct((block, 4, local_units), f32),
-            jax.ShapeDtypeStruct((4, local_units), f32),
-            jax.ShapeDtypeStruct((dec_rows, vocab), f32),
-            jax.ShapeDtypeStruct((1, vocab), f32),
+            pltpu.VMEM((1, 1), f32),
+            pltpu.VMEM((vocab, width), f32),
+            pltpu.VMEM((width, 4, local_units), f32),
+            pltpu.VMEM((block, 4, local_units), f32),
+            pltpu.VMEM((4, local_units), f32),
+            pltpu.VMEM((dec_rows, vocab), f32),
+            pltpu.VMEM((1, vocab), f32),
         ],
         in_specs=[vmem] * 4 + [anywhere] * 2 + [vmem] * 3,
-        out_specs=[anywhere] * 7,
+        out_specs=[vmem] * 7,
         scratch_shapes=[
             pltpu.VMEM((block, 4, local_units), bf16),
             pltpu.VMEM((width, 4, local_units), bf16),
-            pltpu.VMEM((block, 4, local_units), f32),
-            pltpu.VMEM((width, 4, local_units), f32),
-            pltpu.VMEM((4, local_units), f32),
-            pltpu.VMEM((1, 1), f32),
-            pltpu.VMEM((1, vocab), f32),
-            pltpu.VMEM((dec_rows, vocab), f32),
-            pltpu.VMEM((vocab, width), f32),
             pltpu.VMEM((2, LANES, row_count), jnp.int32),
             pltpu.VMEM((row_count, LANES), jnp.int32),
             pltpu.VMEM((2, 4, block, units), bf16),
@@ -1152,7 +1121,6 @@
             pltpu.VMEM((dec_rows, vocab_pad), bf16),
             pltpu.VMEM((dec_rows, vocab_pad), bf16),
             pltpu.SemaphoreType.DMA((PIECES + 2,)),
-            pltpu.SemaphoreType.DMA((2 * SUB + 6,)),
             sems(1),
             sems(3, PIECES + 1),
             sems(4, PIECES + 1),
@@ -1176,7 +1144,7 @@
             sems(2),
         ],
         compiler_params=pltpu.CompilerParams(
-            collective_id=0, has_side_effects=True, vmem_limit_bytes=62 << 20
+            collective_id=0, has_side_effects=True, vmem_limit_bytes=60 << 20
         ),
     )(
         char_ids.T,
@@ -1190,20 +1158,15 @@
         decoder_bias,
     )
     results = [loss, emb_grad, in_grad, rec_grad, bias_grad, dec_grad, dec_bias_grad]
-    parts = 2
-    blocks = [
-        pl.BlockSpec((each.shape[0] // parts,) + each.shape[1:], lambda i: (i, 0, 0))
-        if each.ndim == 3
-        else pl.BlockSpec(each.shape, lambda i: (0, 0))
-        for each in results
-    ]
+    results = [pltpu.with_memory_space_constraint(each, pltpu.VMEM) for each in results]
     loss, emb_grad, in_grad, rec_grad, bias_grad, dec_grad, dec_bias_grad = pl.pallas_call(
         hand_over,
         out_shape=[jax.ShapeDtypeStruct(each.shape, f32) for each in results[:-1]]
         + [jax.ShapeDtypeStruct((vocab,), f32)],
-        grid=(parts,),
-        in_specs=blocks,
-        out_specs=blocks[:-1] + [pl.BlockSpec((vocab,), lambda i: (0,))],
+        in_specs=[vmem] * 7,
+        out_specs=[anywhere] * 7,
+        scratch_shapes=[pltpu.VMEM((vocab,), f32), pltpu.SemaphoreType.DMA((7,))],
+        compiler_params=pltpu.CompilerParams(vmem_limit_bytes=2 << 20),
     )(*results)
     return (
         loss.reshape(()),

time: 201 us -> 200 us (level)
  no operation moved by 1% of the time
where the time goes in v5:
time: 200 us; the launch traced here: 199 us
  Pallas kernels  199 us (100%)
    pallas_call x1, Pallas kernels, grouped(): pl.pallas_call(functools.partial(layer_kernel, dims), out_shape=[pltpu.VM...  196 us

profile of v5, /device:TPU:1, one launch (start us, length us, event | category | flops | bytes accessed | tf_op | source)
XLA Modules:
  0.0 199.4 jit_solution(12158709261230755432)
XLA Ops:
  0.6 196.2 %shard_map.144 = (f32[1,1]{1,0:T(1,128)}, f32[275,100]{1,0:T(8,128)S(1)}, f32[100,4,512]{2,1,0:T(4,128)S(1)}, f32[256,4,512]{2,1,0:T(4,128)S(1)}, f32[4,512]{1,0...) custom-call(s32[6,128]{1,0:T(8,128)} %bitcast.7, s32[6,128]{1,0:T(8,128)} %bitcast.8, s32[6,128]{1,0:T(8,128)} %bitcast.9, ...), custom_call_target="tpu_custom_call" | custom-call | tf_op jit(solution)/shard_map/pallas_call | solution.py:1055
  196.8 2.4 %shard_map.145 = (f32[1,1]{1,0:T(1,128)}, f32[275,100]{1,0:T(8,128)}, f32[100,4,512]{2,1,0:T(4,128)}, f32[256,4,512]{2,1,0:T(4,128)}, f32[4,512]{1,0:T(4,128)}, /*index=5*/f32[64,275]{1,0:T(8,128)}, f32[275]{0:T(512)}) custom-call(f32[1,1]{1,0:T(1,128)} %get-tuple-element.21.refs_0_, f32[275,100]{1,0:T(8,128)S(1)} %get-tuple-element.22.refs_1_, ...), custom_call_target="tpu_custom_call" | custom-call | tf_op jit(solution)/shard_map/pallas_call | solution.py:1162

commit v6 on v5

--- a/solution.py
+++ b/solution.py
@@ -19,7 +19,7 @@
 SPLIT = 2
 PIECES = 8
 LAG = 2
-EARLY = 3
+EARLY = 2
 SUB = 4
 
 
@@ -108,6 +108,7 @@
     emb_part,
     emb_in,
     emb_sums,
+    emb_pairs,
     emb_full,
     dec_part,
     dec_x_out,
@@ -875,14 +876,20 @@
             :, k * LANES : (k + 1) * LANES
         ]
     spot = emb_sums.at[place(0)]
-    emb2 = [copy(spot, spot, emb2_sem, (j,), (flips, 0)) for j, flips in enumerate(OTHERS)]
-    for each in emb2:
-        each.start()
+    emb2 = [copy(spot, spot, emb2_sem, (0,), (1, 0))]
+    emb2[0].start()
     weight_grad(2, 1)
     pass_piece(7)
     send_eighth(6, 10)
     weight_grad(3, 0)
     weight_grad(3, 1)
+
+    spot = emb_sums.at[place(1)]
+    copy(spot, spot, emb2_sem, (0,), (1, 0)).wait_recv()
+    emb_pairs[z_high] = emb_sums[z_high * 2] + emb_sums[z_high * 2 + 1]
+    spot = emb_pairs.at[z_high]
+    emb2.append(copy(spot, spot, emb2_sem, (1,), (4, 0)))
+    emb2[1].start()
 
     giw_z.wait_recv()
     gate_at = x_at * 2 + z_high
@@ -904,10 +911,9 @@
     send_eighth(7, 11)
     pass_piece(9)
     pass_z(8)
-    for j, flips in enumerate(OTHERS):
-        spot = emb_sums.at[place(flips)]
-        copy(spot, spot, emb2_sem, (j,), (flips, 0)).wait_recv()
-    sums = (emb_sums[0] + emb_sums[1]) + (emb_sums[2] + emb_sums[3])
+    spot = emb_pairs.at[1 - z_high]
+    copy(spot, spot, emb2_sem, (1,), (4, 0)).wait_recv()
+    sums = emb_pairs[0] + emb_pairs[1]
     emb_full[own] = sums[:emb_rows]
     spot = emb_full.at[own]
     emb3 = [copy(spot, spot, emb3_sem, (j,), flips) for j, flips in enumerate(GROUP)]
@@ -1114,6 +1120,7 @@
             pltpu.VMEM((8, emb_rows, LANES), f32),
             pltpu.VMEM((8, emb_rows, LANES), f32),
             pltpu.VMEM((4, emb_rows + 8, LANES), f32),
+            pltpu.VMEM((2, emb_rows + 8, LANES), f32),
             pltpu.VMEM((8, emb_rows, LANES), f32),
             pltpu.VMEM((2, 2, dec_rows, vocab_pad), f32),
             pltpu.VMEM((2, dec_rows, vocab_pad), bf16),
@@ -1139,7 +1146,7 @@
             sems(3, 2, SUB),
             sems(8),
             sems(7),
-            sems(3),
+            sems(2),
             sems(7),
             sems(2),
         ],

time: 200 us -> 199 us (level)
  Pallas kernels: 199 us -> 196 us
    pallas_call x1, Pallas kernels: 196 us -> 194 us  [grouped(): pl.pallas_call(functools.partial(layer_kernel, dims), out_shape=[pltpu.VM...]
where the time goes in v6:
time: 199 us; the launch traced here: 197 us
  Pallas kernels  196 us (98%)
    pallas_call x1, Pallas kernels, grouped(): pl.pallas_call(functools.partial(layer_kernel, dims), out_shape=[pltpu.VM...  194 us

profile of v6, /device:TPU:1, one launch (start us, length us, event | category | flops | bytes accessed | tf_op | source)
XLA Modules:
  0.0 196.9 jit_solution(16221953134398174596)
XLA Ops:
  0.6 193.7 %shard_map.144 = (f32[1,1]{1,0:T(1,128)}, f32[275,100]{1,0:T(8,128)S(1)}, f32[100,4,512]{2,1,0:T(4,128)S(1)}, f32[256,4,512]{2,1,0:T(4,128)S(1)}, f32[4,512]{1,0...) custom-call(s32[6,128]{1,0:T(8,128)} %bitcast.7, s32[6,128]{1,0:T(8,128)} %bitcast.8, s32[6,128]{1,0:T(8,128)} %bitcast.9, ...), custom_call_target="tpu_custom_call" | custom-call | tf_op jit(solution)/shard_map/pallas_call | solution.py:1061
  194.3 2.4 %shard_map.145 = (f32[1,1]{1,0:T(1,128)}, f32[275,100]{1,0:T(8,128)}, f32[100,4,512]{2,1,0:T(4,128)}, f32[256,4,512]{2,1,0:T(4,128)}, f32[4,512]{1,0:T(4,128)}, /*index=5*/f32[64,275]{1,0:T(8,128)}, f32[275]{0:T(512)}) custom-call(f32[1,1]{1,0:T(1,128)} %get-tuple-element.21.refs_0_, f32[275,100]{1,0:T(8,128)S(1)} %get-tuple-element.22.refs_1_, ...), custom_call_target="tpu_custom_call" | custom-call | tf_op jit(solution)/shard_map/pallas_call | solution.py:1169
